TPU v7x, 128 devices: a whole 4x4x4 slice. The times are simulated.
128 devices in a mesh: rep: 32 (over y, z, core), shard: 4 (over x).
Axes of the slice: x: 4, y: 4, z: 4, core: 2. Of those that a mesh axis runs over, the one named last changes fastest.
Arguments:
- grads: bfloat16 [32, 16777216], P('rep', 'shard'), may hold values from -64 to 64
Outputs:
- aggregate: bfloat16 [16777216], P('shard')
- weights: float32 [32], replicated
All inputs are finite; a program needn't handle non-finite values.
Results may differ from a plain program's by a relative error of at most 0.0034.
Values may be sent and summed in bfloat16 or wider, within the bound.
No kernel may reach another device: no remote copies, remote signals or barrier semaphores. Data moves between devices by JAX's collectives and lax.ppermute only.
A program may use at most 128 MiB of HBM per device.

v0:
```python
import jax
import jax.numpy as jnp
from jax import lax
from jax.sharding import PartitionSpec as P

ITERS = 4


def weiszfeld(gram, total):
    count = gram.shape[0]
    diag = jnp.diagonal(gram)
    weights = jnp.full((count,), 1.0 / count, dtype=jnp.float32)
    for step in range(ITERS):
        query = jnp.dot(gram, weights, precision=lax.Precision.HIGHEST)
        spread = jnp.dot(weights, query, precision=lax.Precision.HIGHEST)
        square = jnp.maximum((diag - 2.0 * query + spread) / total, 0.0)
        inverse = 1.0 / jnp.sqrt(square + 1e-06)
        weights = inverse / jnp.sum(inverse)
    return weights


def body(grads):
    blocks = lax.all_to_all(grads, "rep", split_axis=1, concat_axis=0, tiled=True)
    partial_value = lax.dot_general(
        blocks, blocks, (((1,), (1,)), ((), ())), preferred_element_type=jnp.float32
    )
    gram = lax.psum(partial_value, ("rep", "shard"))
    total = grads.shape[1] * lax.axis_size("shard")
    weights = weiszfeld(gram, total)
    coeffs = weights.astype(jnp.bfloat16)
    local = jnp.dot(coeffs, blocks, preferred_element_type=jnp.float32).astype(jnp.bfloat16)
    aggregate = lax.all_gather(local, "rep", axis=0, tiled=True)
    return (aggregate, weights)


def solution(mesh):
    placed = (P("rep", "shard"),)
    return jax.shard_map(
        body, mesh=mesh, in_specs=placed, out_specs=(P("shard"), P()), check_vma=False
    )
```

profile of v0, /device:TPU:1, one launch (start us, length us, event | category | flops | bytes accessed | tf_op | source)
XLA Modules:
  0.0 410.3 jit_solution(12220618487178362013)
XLA Ops:
  7.2 0.5 broadcast.80
  7.7 50.6 %reduce.8 = bf16[32,131072]{1,0:T(8,128)(2,1)} reduce(bf16[32,1,131072]{2,1,0:T(2,128)(2,1)} %bitcast.43, bf16[]{:T(256)} %broadcast.80), dimensions={1}, to_apply=%bitcast.29.reduce_sub_computation | reduce | bytes 16777218
  58.3 11.0 %reshape.38 = bf16[32,2,65536]{2,1,0:T(2,128)(2,1)} reshape(bf16[32,131072]{1,0:T(8,128)(2,1)} %reduce.8) | data formatting | bytes 16777216
  69.3 9.7 %all-to-all-start = ((bf16[32,2,65536]{2,1,0:T(2,128)(2,1)}), bf16[32,2,65536]{2,1,0:T(2,128)(2,1)}, u32[]{:S(2)}, u32[]{:S(2)}) async-start(bf16[32,2,65536]{2,1,0:T(2,128)(2,1)} %reshape.38), calls=%async_computation | async-start | bytes 16777216 | tf_op jit(solution)/shard_map/all_to_all | solution.py:23
  78.9 0.0 all-gather.2.cloned.1.call-start
  79.0 108.5 %all-to-all-done = bf16[32,2,65536]{2,1,0:T(2,128)(2,1)} async-done(((bf16[32,2,65536]{2,1,0:T(2,128)(2,1)}), bf16[32,2,65536]{2,1,0:T(2,128)(2,1)}, u32[]{:S(2)}, u32[]{:S(2)}) %all-to-all-start) | async-done | bytes 8388640 | tf_op jit(solution)/shard_map/all_to_all | solution.py:23
  187.5 23.4 %reshape.39 = bf16[32,1,131072]{2,1,0:T(2,128)(2,1)} reshape(bf16[32,2,65536]{2,1,0:T(2,128)(2,1)} %all-to-all-done) | data formatting | bytes 16777216
  210.9 28.1 %fusion.2 = f32[32,32]{1,0:T(8,128)S(1)} fusion(bf16[1,32,131072]{2,0,1:T(2,128)(2,1)} %bitcast.41), kind=kOutput, calls=%fused_computation.3 | convolution fusion | flops 268435456 | bytes 8392704 | tf_op jit(solution)/shard_map/dot_general | solution.py:24
  239.0 79.2 %psum.7 = f32[32,32]{1,0:T(8,128)S(1)} all-reduce(f32[32,32]{1,0:T(8,128)S(1)} %fusion.2), channel_id=1, replica_groups=mesh['rep'=32,'shard'=4] {'rep','shard'}, use_global_device_ids=true, to_apply=%region_0.0 | all-reduce | flops 1024 | bytes 8192 | tf_op jit(solution)/shard_map/psum | solution.py:27
  318.2 0.7 multiply_reduce_fusion.3
  319.0 0.7 gather_fusion
  319.7 1.3 fusion.16
  320.9 1.4 multiply_reduce_fusion.2
  322.3 1.3 fusion.15
  323.6 1.4 multiply_reduce_fusion.1
  325.0 1.3 fusion.14
  326.2 1.4 multiply_reduce_fusion
  327.6 1.3 fusion.13
  328.9 0.6 broadcast_divide_fusion
  329.5 0.0 copy-start
  329.5 14.9 %fusion = f32[1,131072]{1,0:T(1,128)S(1)} fusion(bf16[1,32,131072]{2,0,1:T(2,128)(2,1)} %bitcast.42, f32[32]{0:T(128)S(1)} %broadcast_divide_fusion), kind=kOutput, calls=%fused_computation.1 | convolution fusion | flops 8388640 | bytes 8913024 | tf_op jit(solution)/shard_map/dot_general | solution.py:31
  344.4 0.7 convert_element_type.7
  345.1 0.0 all-gather.2.cloned.1.call-update
  345.1 51.3 %all-gather.2.cloned.1.call-done = bf16[4194304]{0:T(1024)(128)(2,1)} async-done(((bf16[131072]{0:T(1024)(128)(2,1)}), bf16[4194304]{0:T(1024)(128)(2,1)}) %all-gather.2.cloned.1.call-update) | async-done | bytes 8388624 | tf_op jit(solution)/shard_map/all_gather | solution.py:32
  396.4 7.1 %copy.21 = bf16[4194304]{0:T(1024)(128)(2,1)} copy(bf16[4194304]{0:T(1024)(128)(2,1)} %all-gather.2.cloned.1.call-done) | data formatting | bytes 16777216
  403.5 0.0 copy-done
  (1 shorter events, 0.0 us)
Async XLA Ops:
  69.3 118.2 %all-to-all-start = ((bf16[32,2,65536]{2,1,0:T(2,128)(2,1)}), bf16[32,2,65536]{2,1,0:T(2,128)(2,1)}, u32[]{:S(2)}, u32[]{:S(2)}) async-start(bf16[32,2,65536]{2,1,0:T(2,128)(2,1)} %reshape.38), calls=%async_computation | async-start | bytes 16777216 | tf_op jit(solution)/shard_map/all_to_all | solution.py:23
  78.9 317.5 %all-gather.2.cloned.1.call-start = ((), (), s32[]{:S(2)}) async-start(), calls=%async_computation.1 | async-start | bytes 8650752 | tf_op jit(solution)/shard_map/all_gather | solution.py:32
  329.5 74.0 %copy-start = (f32[32]{0:T(128)}, f32[32]{0:T(128)S(1)}, u32[]{:S(2)}) copy-start(f32[32]{0:T(128)S(1)} %broadcast_divide_fusion) | copy-start | bytes 388
Sparse Core Ops, SparseCore 0:
  345.2 51.0 all-gather.1
where the time goes:
time: 411 us; the launch traced here: 410 us
  waiting for transfers between devices  160 us (39%)
  blocking collectives  79.2 us (19%)
  other arithmetic  57 us (14%)
  matrix products  47.9 us (12%)
  local copies, waits for them, and re-layouts  42.7 us (10%)
  between operations  14.1 us (3%)
  starting transfers between devices  9.7 us (2%)
    all_to_all x1, waiting for transfers between devices, body(): lax.all_to_all(grads, 'rep', split_axis=1, concat_axis=0, tiled=True)  108 us
    psum x1, blocking collectives, body(): gram = lax.psum(partial_value, ('rep', 'shard'))  79.2 us
    all_gather x1, waiting for transfers between devices, body(): aggregate = lax.all_gather(local, 'rep', axis=0, tiled=True)  51.3 us
    unnamed x1, other arithmetic  50.6 us
    unnamed x6, local copies, waits for them, and re-layouts  42 us
    dot_general x1, matrix products, body(): lax.dot_general(blocks, blocks, (((1,), (1,)), ((), ())), preferred_eleme...  28.1 us
    dot_general x1, matrix products, body(): jnp.dot(coeffs, blocks, preferred_element_type=jnp.float32)  14.9 us
    all_to_all x1, starting transfers between devices, body(): lax.all_to_all(grads, 'rep', split_axis=1, concat_axis=0, tiled=True)  9.66 us
  transfers between devices with their start and end apart: 2, of which 2 were waited for; matrix products, arithmetic and copies ran while one was open for 0% of the time, Pallas kernels for 0%

commit v1 on v0

v1 whole, which is shorter than its diff:
```python
import functools

import jax
import jax.numpy as jnp
from jax import lax
from jax.experimental import pallas as pl
from jax.experimental.pallas import tpu as pltpu
from jax.sharding import PartitionSpec as P

ITERS = 4
LANES = 128
PACK = 16
VMEM = 48 * 1024 * 1024


def compact_kernel(x_ref, o_ref):
    o_ref[...] = x_ref[...].reshape(o_ref.shape)


def compact(grads, steps):
    size = grads.shape[1]
    rows = size // LANES
    return pl.pallas_call(
        compact_kernel,
        grid=(steps,),
        in_specs=[pl.BlockSpec((1, size // steps), lambda i: (0, i))],
        out_specs=pl.BlockSpec((rows // steps, LANES), lambda i: (i, 0)),
        out_shape=jax.ShapeDtypeStruct((rows, LANES), grads.dtype),
        compiler_params=pltpu.CompilerParams(vmem_limit_bytes=VMEM),
        cost_estimate=pl.CostEstimate(flops=0, bytes_accessed=6 * size, transcendentals=0),
    )(grads)


def gram_kernel(steps, x_ref, o_ref, total):
    step = pl.program_id(0)
    count, rows, _ = x_ref.shape
    wide = count * PACK
    left = jnp.concatenate(
        [x_ref[:, j * PACK : (j + 1) * PACK, :].reshape(wide, LANES) for j in range(rows // PACK)], axis=1
    )
    product = lax.dot_general(left, left, (((1,), (1,)), ((), ())), preferred_element_type=jnp.float32)

    @pl.when(step == 0)
    def _():
        total[...] = product

    @pl.when(step > 0)
    def _():
        total[...] += product

    @pl.when(step == steps - 1)
    def _():
        i = lax.broadcasted_iota(jnp.int32, (wide, wide), 0)
        j = lax.broadcasted_iota(jnp.int32, (wide, wide), 1)
        kept = jnp.where(i % PACK == j % PACK, total[...], 0.0)
        folded = kept.reshape(count, PACK, wide).sum(axis=1)
        k = lax.broadcasted_iota(jnp.int32, (wide, LANES), 0)
        s = lax.broadcasted_iota(jnp.int32, (wide, LANES), 1)
        fold = jnp.where(k // PACK == s % count, 1.0, 0.0)
        spread = jnp.dot(folded, fold, precision=lax.Precision.HIGHEST, preferred_element_type=jnp.float32)
        r = lax.broadcasted_iota(jnp.int32, (count, LANES), 0)
        t = lax.broadcasted_iota(jnp.int32, (count, LANES), 1)
        kept = jnp.where(t // count == r // 8, spread, 0.0)
        o_ref[...] = kept.reshape(count // 8, 8, LANES).sum(axis=0)


def partial_gram(blocks, steps):
    count, rows, _ = blocks.shape
    wide = count * PACK
    return pl.pallas_call(
        functools.partial(gram_kernel, steps),
        grid=(steps,),
        in_specs=[pl.BlockSpec((count, rows // steps, LANES), lambda i: (0, i, 0))],
        out_specs=pl.BlockSpec((8, LANES), lambda i: (0, 0)),
        out_shape=jax.ShapeDtypeStruct((8, LANES), jnp.float32),
        scratch_shapes=[pltpu.VMEM((wide, wide), jnp.float32)],
        compiler_params=pltpu.CompilerParams(vmem_limit_bytes=VMEM),
    )(blocks)


def aggregate_kernel(total, g_ref, x_ref, o_ref, w_ref, coeffs):
    count = x_ref.shape[0]

    @pl.when(pl.program_id(0) == 0)
    def _():
        gram = g_ref[...].sum(axis=0)
        gram = jnp.concatenate([gram] * (count // 8), axis=0)
        r = lax.broadcasted_iota(jnp.int32, (count, LANES), 0)
        t = lax.broadcasted_iota(jnp.int32, (count, LANES), 1)
        gram = jnp.where(t // count == r // 8, gram, 0.0)
        same = (t % count == r).astype(jnp.float32)
        diag = jnp.sum(gram * same, axis=1, keepdims=True)
        weights = jnp.full((count, 1), 1.0 / count, jnp.float32)
        for _ in range(ITERS):
            across = jnp.sum(same * weights, axis=0, keepdims=True)
            query = jnp.sum(gram * across, axis=1, keepdims=True)
            spread = jnp.sum(weights * query, axis=0, keepdims=True)
            square = jnp.maximum((diag - 2.0 * query + spread) / total, 0.0)
            inverse = 1.0 / jnp.sqrt(square + 1e-06)
            weights = inverse / jnp.sum(inverse, axis=0, keepdims=True)
        w_ref[...] = jnp.sum(same * weights, axis=0, keepdims=True)
        coeffs[...] = jnp.broadcast_to(weights.astype(jnp.bfloat16).astype(jnp.float32), (count, LANES))

    rows = x_ref.shape[1]
    piece = 32
    for k in range(rows // piece):
        at = slice(k * piece, (k + 1) * piece)
        parts = [None] * 4
        for r in range(count):
            term = x_ref[r, at, :].astype(jnp.float32) * coeffs[r : r + 1, :]
            parts[r % 4] = term if parts[r % 4] is None else parts[r % 4] + term
        o_ref[at, :] = ((parts[0] + parts[1]) + (parts[2] + parts[3])).astype(o_ref.dtype)


def aggregate_blocks(grams, blocks, total, steps):
    count, rows, _ = blocks.shape
    return pl.pallas_call(
        functools.partial(aggregate_kernel, float(total)),
        grid=(steps,),
        in_specs=[
            pl.BlockSpec(grams.shape, lambda i: (0, 0, 0)),
            pl.BlockSpec((count, rows // steps, LANES), lambda i: (0, i, 0)),
        ],
        out_specs=[
            pl.BlockSpec((rows // steps, LANES), lambda i: (i, 0)),
            pl.BlockSpec((1, LANES), lambda i: (0, 0)),
        ],
        out_shape=[
            jax.ShapeDtypeStruct((rows, LANES), blocks.dtype),
            jax.ShapeDtypeStruct((1, LANES), jnp.float32),
        ],
        scratch_shapes=[pltpu.VMEM((count, LANES), jnp.float32)],
        compiler_params=pltpu.CompilerParams(vmem_limit_bytes=VMEM),
    )(grams, blocks)


def body(grads):
    count = lax.axis_size("rep")
    total = grads.shape[1] * lax.axis_size("shard")
    slab = compact(grads, 16).reshape(count, -1, LANES)
    blocks = lax.all_to_all(slab, "rep", split_axis=0, concat_axis=0, tiled=True)
    gram = partial_gram(blocks, 8)
    everyone = count * lax.axis_size("shard")
    grams = lax.all_to_all(
        jnp.broadcast_to(gram[None], (everyone, 8, LANES)), ("rep", "shard"), 0, 0, tiled=True
    )
    local, weights = aggregate_blocks(grams, blocks, total, 8)
    aggregate = lax.all_gather(local.reshape(-1), "rep", axis=0, tiled=True)
    return (aggregate, weights[0, :count])


def solution(mesh):
    placed = (P("rep", "shard"),)
    return jax.shard_map(
        body, mesh=mesh, in_specs=placed, out_specs=(P("shard"), P()), check_vma=False
    )
```

time: 411 us -> 229 us (0.56)
  waiting for transfers between devices: 160 us -> 48.4 us
  other arithmetic: 57 us -> 0 us
  matrix products: 47.9 us -> 0 us
  blocking collectives: 79.2 us -> 125 us
  local copies, waits for them, and re-layouts: 42.7 us -> 7.65 us
  Pallas kernels: 0 us -> 32.6 us
  starting transfers between devices: 9.7 us -> 0.04 us
    all_to_all x0 -> x2, blocking collectives: none -> 125 us  [the longest x1 105 us: body(): lax.all_to_all(slab, 'rep', split_axis=0, concat_axis=0, tiled=True)]
    all_to_all x1 -> x0, waiting for transfers between devices: 108 us -> none  [body(): lax.all_to_all(grads, 'rep', split_axis=1, concat_axis=0, tiled=True)]
    psum x1 -> x0, blocking collectives: 79.2 us -> none  [body(): gram = lax.psum(partial_value, ('rep', 'shard'))]
    unnamed x1 -> x0, other arithmetic: 50.6 us -> none
    dot_general x6 -> x0, matrix products: 47.9 us -> none  [the longest x1 28.1 us: body(): lax.dot_general(blocks, blocks, (((1,), (1,)), ((), ())), preferred_eleme...]
    unnamed x6 -> x1, local copies, waits for them, and re-layouts: 42 us -> 7.1 us
    pallas_call x0 -> x3, Pallas kernels: none -> 32.6 us  [the longest x1 14.8 us: compact(): pl.pallas_call(compact_kernel, grid=(steps,), in_specs=[pl.BlockSpec((1,...]
    all_to_all x1 -> x0, starting transfers between devices: 9.66 us -> none  [body(): lax.all_to_all(grads, 'rep', split_axis=1, concat_axis=0, tiled=True)]
  transfers between devices with their start and end apart: 2 -> 1, of which waited for: 2 -> 1; matrix products, arithmetic and copies ran while one was open for 0% -> 0% of each run, Pallas kernels for 0% -> 0%
where the time goes in v1:
time: 229 us; the launch traced here: 228 us
  blocking collectives  125 us (55%)
  waiting for transfers between devices  48.4 us (21%)
  Pallas kernels  32.6 us (14%)
  between operations  14 us (6%)
  local copies, waits for them, and re-layouts  7.65 us (3%)
    all_to_all x1, blocking collectives, body(): lax.all_to_all(slab, 'rep', split_axis=0, concat_axis=0, tiled=True)  105 us
    all_gather x1, waiting for transfers between devices, body(): aggregate = lax.all_gather(local.reshape(-1), 'rep', axis=0, tiled=True)  48.4 us
    all_to_all x1, blocking collectives, body(): lax.all_to_all(jnp.broadcast_to(gram[None], (everyone, 8, LANES)), ('rep'...  19.8 us
    pallas_call x1, Pallas kernels, compact(): pl.pallas_call(compact_kernel, grid=(steps,), in_specs=[pl.BlockSpec((1,...  14.8 us
    pallas_call x1, Pallas kernels, partial_gram(): pl.pallas_call(functools.partial(gram_kernel, steps), grid=(steps,), in_s...  9.85 us
    pallas_call x1, Pallas kernels, aggregate_blocks(): pl.pallas_call(functools.partial(aggregate_kernel, float(total)), grid=(s...  7.92 us
    unnamed x1, local copies, waits for them, and re-layouts  7.1 us
  transfers between devices with their start and end apart: 1, of which 1 were waited for; matrix products, arithmetic and copies ran while one was open for 0% of the time, Pallas kernels for 0%

profile of v1, /device:TPU:1, one launch (start us, length us, event | category | flops | bytes accessed | tf_op | source)
XLA Modules:
  0.0 227.7 jit_solution(13360302976487172066)
XLA Ops:
  7.2 0.0 all-gather.2.cloned.1.call-start
  7.2 14.8 %shard_map.30 = bf16[32768,128]{1,0:T(8,128)(2,1)} custom-call(bf16[1,4194304]{1,0:T(2,128)(2,1)} %x_ref.1), custom_call_target="tpu_custom_call" | custom-call | bytes 25165824 | tf_op jit(solution)/shard_map/pallas_call | solution.py:23
  22.0 105.3 %all_to_all.10.x_ref = bf16[32,1024,128]{2,1,0:T(8,128)(2,1)} all-to-all(bf16[32,1024,128]{2,1,0:T(8,128)(2,1)} %bitcast.4), channel_id=1, replica_groups=mesh['rep'=32,'shard'=4] {'rep'}, dimensions={0} | all-to-all | bytes 16777216 | tf_op jit(solution)/shard_map/all_to_all | solution.py:141
  127.3 9.8 %shard_map.31 = f32[8,128]{1,0:T(8,128)S(1)} custom-call(bf16[32,1024,128]{2,1,0:T(8,128)(2,1)} %all_to_all.10.x_ref), custom_call_target="tpu_custom_call" | custom-call | tf_op jit(solution)/shard_map/pallas_call | solution.py:70
  137.2 19.8 %all_to_all.11.g_ref = f32[128,8,128]{2,1,0:T(8,128)S(1)} all-to-all(f32[128,8,128]{2,1,0:T(8,128)S(1)} %broadcast_in_dim.2), channel_id=1, replica_groups=mesh['rep'=32,'shard'=4] {'rep','shard'}, dimensions={0} | all-to-all | bytes 1048576 | tf_op jit(solution)/shard_map/all_to_all | solution.py:144
  157.0 7.9 %shard_map.32 = (bf16[1024,128]{1,0:T(8,128)(2,1)}, f32[1,128]{1,0:T(1,128)S(1)}) custom-call(f32[128,8,128]{2,1,0:T(8,128)S(1)} %all_to_all.11.g_ref, bf16[32,1024,128]{2,1,0:T(8,128)(2,1)} %all_to_all.10.x_ref), custom_call_target="tpu_custom_call" | custom-call | tf_op jit(solution)/shard_map/pallas_call | solution.py:117
  164.9 0.0 all-gather.2.cloned.1.call-update
  164.9 0.5 slice_bitcast_fusion
  165.4 48.4 %all-gather.2.cloned.1.call-done = bf16[4194304]{0:T(1024)(128)(2,1)} async-done(((bf16[131072]{0:T(1024)(128)(2,1)}), bf16[4194304]{0:T(1024)(128)(2,1)}) %all-gather.2.cloned.1.call-update) | async-done | bytes 8388624 | tf_op jit(solution)/shard_map/all_gather | solution.py:148
  213.8 7.1 %copy.4 = bf16[4194304]{0:T(1024)(128)(2,1)} copy(bf16[4194304]{0:T(1024)(128)(2,1)} %all-gather.2.cloned.1.call-done) | data formatting | bytes 16777216
  (1 shorter events, 0.0 us)
Async XLA Ops:
  7.2 206.6 %all-gather.2.cloned.1.call-start = ((), (), s32[]{:S(2)}) async-start(), calls=%async_computation.2 | async-start | bytes 8650752 | tf_op jit(solution)/shard_map/all_gather | solution.py:148
Sparse Core Ops, SparseCore 0:
  165.0 48.7 all-gather.1

commit v2 on v0

v2 whole, which is shorter than its diff:
```python
import functools

import jax
import jax.numpy as jnp
from jax import lax
from jax.experimental import pallas as pl
from jax.experimental.pallas import tpu as pltpu
from jax.sharding import PartitionSpec as P

ITERS = 4
LANES = 128
PACK = 16
SIDE = 4
CORES = 2
COUNT = SIDE * SIDE * CORES
MIB = 1024 * 1024
ANY = pl.BlockSpec(memory_space=pl.ANY)


def compact_kernel(parts, piece, x_ref, o_ref, wide, packed, in_sems, out_sems):
    size = x_ref.shape[1] // parts
    rows = size // LANES
    loads, stores = [], []
    for i in range(parts):
        loads.append(
            pltpu.make_async_copy(x_ref.at[:, pl.ds(i * size, size)], wide.at[:, pl.ds(i * size, size)], in_sems.at[i])
        )
        stores.append(
            pltpu.make_async_copy(packed.at[pl.ds(i * rows, rows)], o_ref.at[pl.ds(i * rows, rows)], out_sems.at[i])
        )
        loads[i].start()
    for i in range(parts):
        loads[i].wait()

        @pl.loop(0, rows // piece)
        def _(j):
            at = pl.multiple_of(i * rows + j * piece, piece)
            values = wide[:, pl.ds(pl.multiple_of(at * LANES, piece * LANES), piece * LANES)]
            packed[pl.ds(at, piece), :] = values.reshape(piece, LANES)

        stores[i].start()
    for store in stores:
        store.wait()


def compact(grads, parts):
    size = grads.shape[1]
    rows = size // LANES
    return pl.pallas_call(
        functools.partial(compact_kernel, parts, 512),
        in_specs=[ANY],
        out_specs=ANY,
        out_shape=jax.ShapeDtypeStruct((rows, LANES), grads.dtype),
        scratch_shapes=[
            pltpu.VMEM((1, size), grads.dtype),
            pltpu.VMEM((rows, LANES), grads.dtype),
            pltpu.SemaphoreType.DMA((parts,)),
            pltpu.SemaphoreType.DMA((parts,)),
        ],
        compiler_params=pltpu.CompilerParams(vmem_limit_bytes=40 * MIB),
        cost_estimate=pl.CostEstimate(flops=0, bytes_accessed=6 * size, transcendentals=0),
    )(grads)


def load_rows(x_ref, held, sems, parts):
    rows = x_ref.shape[1] // parts
    loads = [
        pltpu.make_async_copy(
            x_ref.at[:, pl.ds(i * rows, rows), :], held.at[:, pl.ds(i * rows, rows), :], sems.at[i]
        )
        for i in range(parts)
    ]
    for load in loads:
        load.start()
    return loads


def fold(total):
    wide = total.shape[0]
    i = lax.broadcasted_iota(jnp.int32, (wide, wide), 0)
    j = lax.broadcasted_iota(jnp.int32, (wide, wide), 1)
    kept = jnp.where(i % PACK == j % PACK, total, 0.0)
    k = lax.broadcasted_iota(jnp.int32, (wide, LANES), 0)
    s = lax.broadcasted_iota(jnp.int32, (wide, LANES), 1)
    pick = jnp.where(k // PACK == s, 1.0, 0.0)
    columns = jnp.dot(kept, pick, precision=lax.Precision.HIGHEST, preferred_element_type=jnp.float32)
    return columns.reshape(wide // PACK, PACK, LANES).sum(axis=1)


def gram_kernel(parts, x_ref, o_ref, held, sems):
    loads = load_rows(x_ref, held, sems, parts)
    count, rows, _ = x_ref.shape
    half = count // 2
    rows = rows // parts
    product = functools.partial(
        lax.dot_general, dimension_numbers=(((1,), (1,)), ((), ())), preferred_element_type=jnp.float32
    )

    def group(first, part):
        return jnp.concatenate(
            [
                held[first : first + half, part * rows + j * PACK : part * rows + (j + 1) * PACK, :].reshape(
                    half * PACK, LANES
                )
                for j in range(rows // PACK)
            ],
            axis=1,
        )

    totals = None
    for part in range(parts):
        loads[part].wait()
        low, high = group(0, part), group(half, part)
        found = (product(low, low), product(high, low), product(high, high))
        totals = found if totals is None else tuple(a + b for a, b in zip(totals, found))
    low_low, high_low, high_high = (fold(t) for t in totals)
    square = jnp.concatenate([high_low, jnp.zeros((LANES - half, LANES), jnp.float32)], axis=0)
    low_high = square.T[:half]
    gram = jnp.concatenate(
        [low_low + pltpu.roll(low_high, half, 1), high_low + pltpu.roll(high_high, half, 1)], axis=0
    )
    for q in range(count // 8):
        part = gram[8 * q : 8 * (q + 1)]
        part = part if q == 0 else pltpu.roll(part, count * q, 1)
        o_ref[...] = part if q == 0 else o_ref[...] + part


def partial_gram(blocks, parts):
    return pl.pallas_call(
        functools.partial(gram_kernel, parts),
        in_specs=[ANY],
        out_shape=jax.ShapeDtypeStruct((8, LANES), jnp.float32),
        scratch_shapes=[pltpu.VMEM(blocks.shape, blocks.dtype), pltpu.SemaphoreType.DMA((parts,))],
        compiler_params=pltpu.CompilerParams(vmem_limit_bytes=32 * MIB),
    )(blocks)


def weiszfeld(grams, count, total):
    gram = grams.sum(axis=0)
    gram = jnp.concatenate([gram] * (count // 8), axis=0)
    r = lax.broadcasted_iota(jnp.int32, (count, LANES), 0)
    t = lax.broadcasted_iota(jnp.int32, (count, LANES), 1)
    gram = jnp.where(t // count == r // 8, gram, 0.0)
    same = (t % count == r).astype(jnp.float32)
    diag = jnp.sum(gram * same, axis=1, keepdims=True)
    weights = jnp.full((count, 1), 1.0 / count, jnp.float32)
    for _ in range(ITERS):
        across = jnp.sum(same * weights, axis=0, keepdims=True)
        query = jnp.sum(gram * across, axis=1, keepdims=True)
        spread = jnp.sum(weights * query, axis=0, keepdims=True)
        square = jnp.maximum((diag - 2.0 * query + spread) / total, 0.0)
        inverse = 1.0 / jnp.sqrt(square + 1e-06)
        weights = inverse / jnp.sum(inverse, axis=0, keepdims=True)
    return weights, same


def aggregate_kernel(total, parts, g_ref, x_ref, o_ref, w_ref, coeffs, held, sems):
    loads = load_rows(x_ref, held, sems, parts)
    count, rows, _ = x_ref.shape
    rows = rows // parts
    weights, same = weiszfeld(g_ref[...], count, total)
    w_ref[...] = jnp.sum(same * weights, axis=0, keepdims=True)
    coeffs[...] = jnp.broadcast_to(weights.astype(jnp.bfloat16).astype(jnp.float32), (count, LANES))
    piece = 32
    for part in range(parts):
        loads[part].wait()

        @pl.loop(0, rows // piece)
        def _(k):
            at = pl.ds(pl.multiple_of(part * rows + k * piece, piece), piece)
            sums = [None] * 4
            for r in range(count):
                term = held[r, at, :].astype(jnp.float32) * coeffs[r : r + 1, :]
                sums[r % 4] = term if sums[r % 4] is None else sums[r % 4] + term
            o_ref[at, :] = ((sums[0] + sums[1]) + (sums[2] + sums[3])).astype(o_ref.dtype)


def aggregate_blocks(grams, blocks, total, parts):
    count, rows, _ = blocks.shape
    return pl.pallas_call(
        functools.partial(aggregate_kernel, float(total), parts),
        in_specs=[pl.BlockSpec(memory_space=pltpu.VMEM), ANY],
        out_shape=[
            jax.ShapeDtypeStruct((rows, LANES), blocks.dtype),
            jax.ShapeDtypeStruct((1, LANES), jnp.float32),
        ],
        scratch_shapes=[
            pltpu.VMEM((count, LANES), jnp.float32),
            pltpu.VMEM(blocks.shape, blocks.dtype),
            pltpu.SemaphoreType.DMA((parts,)),
        ],
        compiler_params=pltpu.CompilerParams(vmem_limit_bytes=32 * MIB),
    )(grams, blocks)


def send(array, first, second):
    pairs = []
    for y in range(SIDE):
        for z in range(SIDE):
            for core in range(CORES):
                dy, dz = (first, second) if core == 0 else (second, first)
                there = (y + dy) % SIDE * SIDE + (z + dz) % SIDE
                pairs.append(((y * SIDE + z) * CORES + core, there * CORES + core))
    return lax.ppermute(array, "rep", pairs)


def swap(array):
    return lax.ppermute(array, "rep", [(i, i ^ 1) for i in range(COUNT)])


def place_kernel(moves, rows, *refs):
    sources, (out, held, in_sems, out_sems) = refs[: len(moves)], refs[-4:]
    me = lax.axis_index("rep")
    y, z, core = me // (SIDE * CORES), me // CORES % SIDE, me % CORES
    loads, stores = [], []
    for source, pieces in zip(sources, moves):
        for at, first, second, swapped in pieces:
            owner = 1 - core if swapped else core
            dy = jnp.where(owner == 0, first, second)
            dz = jnp.where(owner == 0, second, first)
            block = ((y - dy + SIDE) % SIDE * SIDE + (z - dz + SIDE) % SIDE) * CORES + owner
            n = len(loads)
            slot = held.at[pl.ds(n * rows, rows)]
            target = out.at[pl.ds(pl.multiple_of(block * rows, rows), rows)]
            loads.append(pltpu.make_async_copy(source.at[pl.ds(at, rows)], slot, in_sems.at[n]))
            stores.append(pltpu.make_async_copy(slot, target, out_sems.at[n]))
    for load in loads:
        load.start()
    for load, store in zip(loads, stores):
        load.wait()
        store.start()
    for store in stores:
        store.wait()


def place(out, rows, sources, moves):
    count = sum(len(m) for m in moves)
    held = count * rows
    args = list(sources) + ([] if out is None else [out])
    return pl.pallas_call(
        functools.partial(place_kernel, moves, rows),
        in_specs=[ANY] * len(args),
        out_specs=ANY,
        out_shape=jax.ShapeDtypeStruct((COUNT * rows, LANES), sources[0].dtype),
        scratch_shapes=[
            pltpu.VMEM((held, LANES), sources[0].dtype),
            pltpu.SemaphoreType.DMA((count,)),
            pltpu.SemaphoreType.DMA((count,)),
        ],
        input_output_aliases={} if out is None else {len(args) - 1: 0},
        compiler_params=pltpu.CompilerParams(vmem_limit_bytes=held * LANES * 2 + 2 * MIB),
        cost_estimate=pl.CostEstimate(flops=0, bytes_accessed=held * LANES * 4, transcendentals=0),
    )(*args)


def gather(own):
    rows = own.shape[0]
    one, three, two = send(own, 1, 0), send(own, 3, 0), send(own, 2, 0)
    upper = jnp.concatenate([own, one])
    lower = jnp.concatenate([three, two])

    def moves(firsts, second, swapped):
        return [(k * rows, first, second, swapped) for k, first in enumerate(firsts)]

    up, low = (0, 1), (3, 2)
    upper_1, upper_3 = send(upper, 0, 1), send(upper, 0, 3)
    lower_1, lower_3 = send(lower, 0, 1), send(lower, 0, 3)
    upper_2, lower_2 = send(upper_1, 0, 1), send(lower_3, 0, 3)
    out = place(
        None,
        rows,
        [upper, lower, swap(upper), swap(lower)],
        [moves(up, 0, False), moves(low, 0, False), moves(up, 0, True), moves(low, 0, True)],
    )
    near = [upper_1, upper_3, lower_1, lower_3]
    layout = [(up, 1), (up, 3), (low, 1), (low, 3)]
    out = place(out, rows, near, [moves(f, s, False) for f, s in layout])
    out = place(out, rows, [swap(a) for a in near], [moves(f, s, True) for f, s in layout])
    far = [upper_2, lower_2]
    layout = [(up, 2), (low, 2)]
    return place(
        out,
        rows,
        far + [swap(a) for a in far],
        [moves(f, s, False) for f, s in layout] + [moves(f, s, True) for f, s in layout],
    )


def body(grads):
    count = lax.axis_size("rep")
    total = grads.shape[1] * lax.axis_size("shard")
    slab = compact(grads, 8).reshape(count, -1, LANES)
    blocks = lax.all_to_all(slab, "rep", split_axis=0, concat_axis=0, tiled=True)
    gram = partial_gram(blocks, 4)
    everyone = count * lax.axis_size("shard")
    grams = lax.all_to_all(
        jnp.broadcast_to(gram[None], (everyone, 8, LANES)), ("rep", "shard"), 0, 0, tiled=True
    )
    local, weights = aggregate_blocks(grams, blocks, total, 4)
    return (gather(local).reshape(-1), weights[0, :count])


def solution(mesh):
    placed = (P("rep", "shard"),)
    return jax.shard_map(
        body, mesh=mesh, in_specs=placed, out_specs=(P("shard"), P()), check_vma=False
    )
```

time: 411 us -> 184 us (0.45)
  waiting for transfers between devices: 160 us -> 18.1 us
  other arithmetic: 57 us -> 0 us
  matrix products: 47.9 us -> 0 us
  blocking collectives: 79.2 us -> 125 us
  local copies, waits for them, and re-layouts: 42.7 us -> 0.65 us
  Pallas kernels: 0 us -> 23.1 us
  between operations: 14.1 us -> 0.76 us
  starting transfers between devices: 9.7 us -> 16 us
    all_to_all x0 -> x2, blocking collectives: none -> 125 us  [the longest x1 105 us: body(): lax.all_to_all(slab, 'rep', split_axis=0, concat_axis=0, tiled=True)]
    all_to_all x1 -> x0, waiting for transfers between devices: 108 us -> none  [body(): lax.all_to_all(grads, 'rep', split_axis=1, concat_axis=0, tiled=True)]
    psum x1 -> x0, blocking collectives: 79.2 us -> none  [body(): gram = lax.psum(partial_value, ('rep', 'shard'))]
    all_gather x1 -> x0, waiting for transfers between devices: 51.3 us -> none  [body(): aggregate = lax.all_gather(local, 'rep', axis=0, tiled=True)]
    unnamed x1 -> x0, other arithmetic: 50.6 us -> none
    dot_general x6 -> x0, matrix products: 47.9 us -> none  [the longest x1 28.1 us: body(): lax.dot_general(blocks, blocks, (((1,), (1,)), ((), ())), preferred_eleme...]
    unnamed x6 -> x2, local copies, waits for them, and re-layouts: 42 us -> 0.04 us
    pallas_call x0 -> x7, Pallas kernels: none -> 23.1 us  [the longest x1 7.1 us: partial_gram(): pl.pallas_call(functools.partial(gram_kernel, parts), in_specs=[ANY], out...]
  transfers between devices with their start and end apart: 2 -> 17, of which waited for: 2 -> 7; matrix products, arithmetic and copies ran while one was open for 0% -> 0% of each run, Pallas kernels for 0% -> 3%
where the time goes in v2:
time: 184 us; the launch traced here: 183 us
  blocking collectives  125 us (68%)
  Pallas kernels  23.1 us (13%)
  waiting for transfers between devices  18.1 us (10%)
  starting transfers between devices  16 us (9%)
    all_to_all x1, blocking collectives, body(): lax.all_to_all(slab, 'rep', split_axis=0, concat_axis=0, tiled=True)  105 us
    all_to_all x1, blocking collectives, body(): lax.all_to_all(jnp.broadcast_to(gram[None], (everyone, 8, LANES)), ('rep'...  19.8 us
    ppermute x9, waiting for transfers between devices, send(): return lax.ppermute(array, 'rep', pairs)  18.1 us
    ppermute x9, starting transfers between devices, send(): return lax.ppermute(array, 'rep', pairs)  9.55 us
    pallas_call x1, Pallas kernels, partial_gram(): pl.pallas_call(functools.partial(gram_kernel, parts), in_specs=[ANY], out...  7.1 us
    pallas_call x4, Pallas kernels, place(): pl.pallas_call(functools.partial(place_kernel, moves, rows), in_specs=[AN...  6.63 us
    ppermute x8, starting transfers between devices, swap(): return lax.ppermute(array, 'rep', [(i, i ^ 1) for i in range(COUNT)])  6.48 us
    pallas_call x1, Pallas kernels, compact(): pl.pallas_call(functools.partial(compact_kernel, parts, 512), in_specs=[A...  6.26 us
  transfers between devices with their start and end apart: 17, of which 7 were waited for; matrix products, arithmetic and copies ran while one was open for 0% of the time, Pallas kernels for 3%

profile of v2, /device:TPU:1, one launch (start us, length us, event | category | flops | bytes accessed | tf_op | source)
XLA Modules:
  0.0 183.4 jit_solution(11772265668604501794)
XLA Ops:
  0.6 6.3 %shard_map.30 = bf16[32768,128]{1,0:T(8,128)(2,1)S(1)} custom-call(bf16[1,4194304]{1,0:T(2,128)(2,1)} %x_ref.1), custom_call_target="tpu_custom_call" | custom-call | bytes 25165824 | tf_op jit(solution)/shard_map/pallas_call | solution.py:49
  6.9 105.0 %all_to_all.10.x_ref = bf16[32,1024,128]{2,1,0:T(8,128)(2,1)S(1)} all-to-all(bf16[32,1024,128]{2,1,0:T(8,128)(2,1)S(1)} %bitcast.4), channel_id=1, replica_groups=mesh['rep'=32,'shard'=4] {'rep'}, dimensions={0} | all-to-all | bytes 16777216 | tf_op jit(solution)/shard_map/all_to_all | solution.py:293
  111.9 7.1 %shard_map.31 = f32[8,128]{1,0:T(8,128)S(1)} custom-call(bf16[32,1024,128]{2,1,0:T(8,128)(2,1)S(1)} %all_to_all.10.x_ref), custom_call_target="tpu_custom_call" | custom-call | tf_op jit(solution)/shard_map/pallas_call | solution.py:129
  119.0 19.8 %all_to_all.11.g_ref = f32[128,8,128]{2,1,0:T(8,128)S(1)} all-to-all(f32[128,8,128]{2,1,0:T(8,128)S(1)} %broadcast_in_dim.2), channel_id=1, replica_groups=mesh['rep'=32,'shard'=4] {'rep','shard'}, dimensions={0} | all-to-all | bytes 1048576 | tf_op jit(solution)/shard_map/all_to_all | solution.py:296
  138.8 3.1 %shard_map.32 = (bf16[1024,128]{1,0:T(8,128)(2,1)S(1)}, f32[1,128]{1,0:T(1,128)S(1)}) custom-call(f32[128,8,128]{2,1,0:T(8,128)S(1)} %all_to_all.11.g_ref, bf16[32,1024,128]{2,1,0:T(8,128)(2,1)S(1)} %all_to_all.10.x_ref), custom_call_target="tpu_custom_call" | custom-call | tf_op jit(solution)/shard_map/pallas_call | solution.py:180
  142.0 0.4 collective-permute-start.3
  142.4 0.5 collective-permute-start.4
  142.9 0.6 collective-permute-start
  143.5 4.0 %collective-permute-done.3 = bf16[1024,128]{1,0:T(8,128)(2,1)S(1)} collective-permute-done((bf16[1024,128]{1,0:T(8,128)(2,1)S(1)}, bf16[1024,128]{1,0:T(8,128)(2,1)S(1)}, u32[]{:S(2)}, u32[]{:S(2)}) %collective-permute-start.3) | collective-permute-done | bytes 262176 | tf_op jit(solution)/shard_map/ppermute | solution.py:204
  147.6 1.9 %collective-permute-done.4 = bf16[1024,128]{1,0:T(8,128)(2,1)S(1)} collective-permute-done((bf16[1024,128]{1,0:T(8,128)(2,1)S(1)}, bf16[1024,128]{1,0:T(8,128)(2,1)S(1)}, u32[]{:S(2)}, u32[]{:S(2)}) %collective-permute-start.4) | collective-permute-done | bytes 262176 | tf_op jit(solution)/shard_map/ppermute | solution.py:204
  149.5 2.0 %collective-permute-start.16 = (bf16[2048,128]{1,0:T(8,128)(2,1)S(1)}, bf16[2048,128]{1,0:T(8,128)(2,1)S(1)}, u32[]{:S(2)}, u32[]{:S(2)}) collective-permute-start(bf16[2048,128]{1,0:T(8,128)(2,1)S(1)} %constant_dynamic-update-slice_fusion.2.refs_1_), channel_id=1, source_target_pairs={{0,4},{4,0},{8,12},{12,8},{16,20},{20,16},{24,28},{28,24},{32,36},... | collective-permute-start | bytes 1572872 | tf_op jit(solution)/shard_map/ppermute | solution.py:208
  151.5 2.5 %collective-permute-start.5 = (bf16[2048,128]{1,0:T(8,128)(2,1)S(1)}, bf16[2048,128]{1,0:T(8,128)(2,1)S(1)}, u32[]{:S(2)}, u32[]{:S(2)}) collective-permute-start(bf16[2048,128]{1,0:T(8,128)(2,1)S(1)} %constant_dynamic-update-slice_fusion.2.refs_1_), channel_id=1, source_target_pairs={{0,24},{4,100},{8,0},{12,108},{16,8},{20,116},{24,16},{28,124},{32... | collective-permute-start | bytes 1572872 | tf_op jit(solution)/shard_map/ppermute | solution.py:204
  154.0 0.2 collective-permute-start.15
  154.2 1.0 collective-permute-start.12
  155.2 1.8 collective-permute-start.10
  156.9 3.2 %collective-permute-done.5.refs_3_ = bf16[2048,128]{1,0:T(8,128)(2,1)S(1)} collective-permute-done((bf16[2048,128]{1,0:T(8,128)(2,1)S(1)}, bf16[2048,128]{1,0:T(8,128)(2,1)S(1)}, u32[]{:S(2)}, u32[]{:S(2)}) %collective-permute-start.5) | collective-permute-done | bytes 524320 | tf_op jit(solution)/shard_map/ppermute | solution.py:204
  160.1 0.6 collective-permute-start.14
  160.7 2.8 %collective-permute-start.6 = (bf16[2048,128]{1,0:T(8,128)(2,1)S(1)}, bf16[2048,128]{1,0:T(8,128)(2,1)S(1)}, u32[]{:S(2)}, u32[]{:S(2)}) collective-permute-start(bf16[2048,128]{1,0:T(8,128)(2,1)S(1)} %collective-permute-done.5.refs_3_), channel_id=1, source_target_pairs={{0,24},{4,100},{8,0},{12,108},{16,8},{20,116},{24,16},{28,124},{32... | collective-permute-start | bytes 1572872 | tf_op jit(solution)/shard_map/ppermute | solution.py:204
  163.5 0.2 collective-permute-done.1.refs_0_
  163.7 5.6 %collective-permute-done.12.refs_2_ = bf16[2048,128]{1,0:T(8,128)(2,1)S(1)} collective-permute-done((bf16[2048,128]{1,0:T(8,128)(2,1)S(1)}, bf16[2048,128]{1,0:T(8,128)(2,1)S(1)}, u32[]{:S(2)}, u32[]{:S(2)}) %collective-permute-start.12) | collective-permute-done | bytes 524320 | tf_op jit(solution)/shard_map/ppermute | solution.py:204
  169.3 1.3 collective-permute-start.9
  170.6 0.0 collective-permute-start.13
  170.6 0.5 collective-permute-start.11
  171.1 0.2 collective-permute-done.6.refs_1_
  171.3 0.6 collective-permute-start.8
  172.0 3.0 %collective-permute-done.2.refs_0_ = bf16[2048,128]{1,0:T(8,128)(2,1)S(1)} collective-permute-done((bf16[2048,128]{1,0:T(8,128)(2,1)S(1)}, bf16[2048,128]{1,0:T(8,128)(2,1)S(1)}, u32[]{:S(2)}, u32[]{:S(2)}) %collective-permute-start.2) | collective-permute-done | bytes 524320 | tf_op jit(solution)/shard_map/ppermute | solution.py:204
  174.9 1.3 collective-permute-start.7
  176.2 0.5 slice_bitcast_fusion
  176.7 1.6 shard_map.33.refs_4_
  178.3 1.7 shard_map.34.refs_4_
  180.0 1.7 shard_map.35.refs_4_
  181.8 1.7 shard_map.36
  (17 shorter events, 0.2 us)
Async XLA Ops:
  142.0 5.6 %collective-permute-start.3 = (bf16[1024,128]{1,0:T(8,128)(2,1)S(1)}, bf16[1024,128]{1,0:T(8,128)(2,1)S(1)}, u32[]{:S(2)}, u32[]{:S(2)}) collective-permute-start(bf16[1024,128]{1,0:T(8,128)(2,1)S(1)} %get-tuple-element.4), channel_id=1, source_target_pairs={{0,96},{4,28},{8,104},{12,4},{16,112},{20,12},{24,120},{28,20},{32... | collective-permute-start | bytes 786440 | tf_op jit(solution)/shard_map/ppermute | solution.py:204
  142.4 7.1 %collective-permute-start.4 = (bf16[1024,128]{1,0:T(8,128)(2,1)S(1)}, bf16[1024,128]{1,0:T(8,128)(2,1)S(1)}, u32[]{:S(2)}, u32[]{:S(2)}) collective-permute-start(bf16[1024,128]{1,0:T(8,128)(2,1)S(1)} %get-tuple-element.4), channel_id=1, source_target_pairs={{0,64},{4,20},{8,72},{12,28},{16,80},{20,4},{24,88},{28,12},{32,96... | collective-permute-start | bytes 786440 | tf_op jit(solution)/shard_map/ppermute | solution.py:204
  142.9 11.1 %collective-permute-start = (bf16[1024,128]{1,0:T(8,128)(2,1)S(1)}, bf16[1024,128]{1,0:T(8,128)(2,1)S(1)}, u32[]{:S(2)}, u32[]{:S(2)}) collective-permute-start(bf16[1024,128]{1,0:T(8,128)(2,1)S(1)} %get-tuple-element.4), channel_id=1, source_target_pairs={{0,32},{4,12},{8,40},{12,20},{16,48},{20,28},{24,56},{28,4},{32,64... | collective-permute-start | bytes 786440 | tf_op jit(solution)/shard_map/ppermute | solution.py:204
  149.5 5.7 %collective-permute-start.16 = (bf16[2048,128]{1,0:T(8,128)(2,1)S(1)}, bf16[2048,128]{1,0:T(8,128)(2,1)S(1)}, u32[]{:S(2)}, u32[]{:S(2)}) collective-permute-start(bf16[2048,128]{1,0:T(8,128)(2,1)S(1)} %constant_dynamic-update-slice_fusion.2.refs_1_), channel_id=1, source_target_pairs={{0,4},{4,0},{8,12},{12,8},{16,20},{20,16},{24,28},{28,24},{32,36},... | collective-permute-start | bytes 1572872 | tf_op jit(solution)/shard_map/ppermute | solution.py:208
  151.5 8.6 %collective-permute-start.5 = (bf16[2048,128]{1,0:T(8,128)(2,1)S(1)}, bf16[2048,128]{1,0:T(8,128)(2,1)S(1)}, u32[]{:S(2)}, u32[]{:S(2)}) collective-permute-start(bf16[2048,128]{1,0:T(8,128)(2,1)S(1)} %constant_dynamic-update-slice_fusion.2.refs_1_), channel_id=1, source_target_pairs={{0,24},{4,100},{8,0},{12,108},{16,8},{20,116},{24,16},{28,124},{32... | collective-permute-start | bytes 1572872 | tf_op jit(solution)/shard_map/ppermute | solution.py:204
  154.0 6.7 %collective-permute-start.15 = (bf16[2048,128]{1,0:T(8,128)(2,1)S(1)}, bf16[2048,128]{1,0:T(8,128)(2,1)S(1)}, u32[]{:S(2)}, u32[]{:S(2)}) collective-permute-start(bf16[2048,128]{1,0:T(8,128)(2,1)S(1)} %constant_dynamic-update-slice_fusion.refs_0_), channel_id=1, source_target_pairs={{0,4},{4,0},{8,12},{12,8},{16,20},{20,16},{24,28},{28,24},{32,36},... | collective-permute-start | bytes 1572872 | tf_op jit(solution)/shard_map/ppermute | solution.py:208
  154.2 9.5 %collective-permute-start.1 = (bf16[2048,128]{1,0:T(8,128)(2,1)S(1)}, bf16[2048,128]{1,0:T(8,128)(2,1)S(1)}, u32[]{:S(2)}, u32[]{:S(2)}) collective-permute-start(bf16[2048,128]{1,0:T(8,128)(2,1)S(1)} %constant_dynamic-update-slice_fusion.refs_0_), channel_id=1, source_target_pairs={{0,8},{4,36},{8,16},{12,44},{16,24},{20,52},{24,0},{28,60},{32,40}... | collective-permute-start | bytes 1572872 | tf_op jit(solution)/shard_map/ppermute | solution.py:204
  154.2 15.1 %collective-permute-start.12 = (bf16[2048,128]{1,0:T(8,128)(2,1)S(1)}, bf16[2048,128]{1,0:T(8,128)(2,1)S(1)}, u32[]{:S(2)}, u32[]{:S(2)}) collective-permute-start(bf16[2048,128]{1,0:T(8,128)(2,1)S(1)} %constant_dynamic-update-slice_fusion.2.refs_1_), channel_id=1, source_target_pairs={{0,8},{4,36},{8,16},{12,44},{16,24},{20,52},{24,0},{28,60},{32,40}... | collective-permute-start | bytes 1572872 | tf_op jit(solution)/shard_map/ppermute | solution.py:204
  155.2 15.4 %collective-permute-start.10 = (bf16[2048,128]{1,0:T(8,128)(2,1)S(1)}, bf16[2048,128]{1,0:T(8,128)(2,1)S(1)}, u32[]{:S(2)}, u32[]{:S(2)}) collective-permute-start(bf16[2048,128]{1,0:T(8,128)(2,1)S(1)} %constant_dynamic-update-slice_fusion.refs_0_), channel_id=1, source_target_pairs={{0,24},{4,100},{8,0},{12,108},{16,8},{20,116},{24,16},{28,124},{32... | collective-permute-start | bytes 1572872 | tf_op jit(solution)/shard_map/ppermute | solution.py:204
  160.1 10.5 %collective-permute-start.14 = (bf16[2048,128]{1,0:T(8,128)(2,1)S(1)}, bf16[2048,128]{1,0:T(8,128)(2,1)S(1)}, u32[]{:S(2)}, u32[]{:S(2)}) collective-permute-start(bf16[2048,128]{1,0:T(8,128)(2,1)S(1)} %collective-permute-done.5.refs_3_), channel_id=1, source_target_pairs={{0,4},{4,0},{8,12},{12,8},{16,20},{20,16},{24,28},{28,24},{32,36},... | collective-permute-start | bytes 1572872 | tf_op jit(solution)/shard_map/ppermute | solution.py:208
  160.7 10.6 %collective-permute-start.6 = (bf16[2048,128]{1,0:T(8,128)(2,1)S(1)}, bf16[2048,128]{1,0:T(8,128)(2,1)S(1)}, u32[]{:S(2)}, u32[]{:S(2)}) collective-permute-start(bf16[2048,128]{1,0:T(8,128)(2,1)S(1)} %collective-permute-done.5.refs_3_), channel_id=1, source_target_pairs={{0,24},{4,100},{8,0},{12,108},{16,8},{20,116},{24,16},{28,124},{32... | collective-permute-start | bytes 1572872 | tf_op jit(solution)/shard_map/ppermute | solution.py:204
  163.7 11.2 %collective-permute-start.2 = (bf16[2048,128]{1,0:T(8,128)(2,1)S(1)}, bf16[2048,128]{1,0:T(8,128)(2,1)S(1)}, u32[]{:S(2)}, u32[]{:S(2)}) collective-permute-start(bf16[2048,128]{1,0:T(8,128)(2,1)S(1)} %collective-permute-done.1.refs_0_), channel_id=1, source_target_pairs={{0,8},{4,36},{8,16},{12,44},{16,24},{20,52},{24,0},{28,60},{32,40}... | collective-permute-start | bytes 1572872 | tf_op jit(solution)/shard_map/ppermute | solution.py:204
  169.3 10.7 %collective-permute-start.9 = (bf16[2048,128]{1,0:T(8,128)(2,1)S(1)}, bf16[2048,128]{1,0:T(8,128)(2,1)S(1)}, u32[]{:S(2)}, u32[]{:S(2)}) collective-permute-start(bf16[2048,128]{1,0:T(8,128)(2,1)S(1)} %collective-permute-done.1.refs_0_), channel_id=1, source_target_pairs={{0,4},{4,0},{8,12},{12,8},{16,20},{20,16},{24,28},{28,24},{32,36},... | collective-permute-start | bytes 1572872 | tf_op jit(solution)/shard_map/ppermute | solution.py:208
  170.6 9.4 %collective-permute-start.13 = (bf16[2048,128]{1,0:T(8,128)(2,1)S(1)}, bf16[2048,128]{1,0:T(8,128)(2,1)S(1)}, u32[]{:S(2)}, u32[]{:S(2)}) collective-permute-start(bf16[2048,128]{1,0:T(8,128)(2,1)S(1)} %collective-permute-done.12.refs_2_), channel_id=1, source_target_pairs={{0,4},{4,0},{8,12},{12,8},{16,20},{20,16},{24,28},{28,24},{32,36},... | collective-permute-start | bytes 1572872 | tf_op jit(solution)/shard_map/ppermute | solution.py:208
  170.6 9.4 %collective-permute-start.11 = (bf16[2048,128]{1,0:T(8,128)(2,1)S(1)}, bf16[2048,128]{1,0:T(8,128)(2,1)S(1)}, u32[]{:S(2)}, u32[]{:S(2)}) collective-permute-start(bf16[2048,128]{1,0:T(8,128)(2,1)S(1)} %collective-permute-done.10.refs_1_), channel_id=1, source_target_pairs={{0,4},{4,0},{8,12},{12,8},{16,20},{20,16},{24,28},{28,24},{32,36},... | collective-permute-start | bytes 1572872 | tf_op jit(solution)/shard_map/ppermute | solution.py:208
  171.3 10.4 %collective-permute-start.8 = (bf16[2048,128]{1,0:T(8,128)(2,1)S(1)}, bf16[2048,128]{1,0:T(8,128)(2,1)S(1)}, u32[]{:S(2)}, u32[]{:S(2)}) collective-permute-start(bf16[2048,128]{1,0:T(8,128)(2,1)S(1)} %collective-permute-done.6.refs_1_), channel_id=1, source_target_pairs={{0,4},{4,0},{8,12},{12,8},{16,20},{20,16},{24,28},{28,24},{32,36},... | collective-permute-start | bytes 1572872 | tf_op jit(solution)/shard_map/ppermute | solution.py:208
  174.9 6.8 %collective-permute-start.7 = (bf16[2048,128]{1,0:T(8,128)(2,1)S(1)}, bf16[2048,128]{1,0:T(8,128)(2,1)S(1)}, u32[]{:S(2)}, u32[]{:S(2)}) collective-permute-start(bf16[2048,128]{1,0:T(8,128)(2,1)S(1)} %collective-permute-done.2.refs_0_), channel_id=1, source_target_pairs={{0,4},{4,0},{8,12},{12,8},{16,20},{20,16},{24,28},{28,24},{32,36},... | collective-permute-start | bytes 1572872 | tf_op jit(solution)/shard_map/ppermute | solution.py:208

commit v3 on v2

v3 whole, which is shorter than its diff:
```python
import functools

import jax
import jax.numpy as jnp
from jax import lax
from jax.experimental import pallas as pl
from jax.experimental.pallas import tpu as pltpu
from jax.sharding import PartitionSpec as P

ITERS = 4
LANES = 128
PACK = 16
SIDE = 4
CORES = 2
COUNT = SIDE * SIDE * CORES
SHORT = 4
MIB = 1024 * 1024
ANY = pl.BlockSpec(memory_space=pl.ANY)
WHOLE = pl.BlockSpec(memory_space=pltpu.VMEM)


def compact_kernel(parts, piece, x_ref, o_ref, wide, sems):
    size = x_ref.shape[1] // parts
    rows = size // LANES
    loads = [
        pltpu.make_async_copy(x_ref.at[:, pl.ds(i * size, size)], wide.at[:, pl.ds(i * size, size)], sems.at[i])
        for i in range(parts)
    ]
    for load in loads:
        load.start()
    for i in range(parts):
        loads[i].wait()

        @pl.loop(0, rows // piece)
        def _(j):
            at = pl.multiple_of(i * rows + j * piece, piece)
            values = wide[:, pl.ds(pl.multiple_of(at * LANES, piece * LANES), piece * LANES)]
            o_ref[pl.ds(at, piece), :] = values.reshape(piece, LANES)


def compact(grads, parts):
    size = grads.shape[1]
    rows = size // LANES
    return pl.pallas_call(
        functools.partial(compact_kernel, parts, 512),
        in_specs=[ANY],
        out_specs=WHOLE,
        out_shape=jax.ShapeDtypeStruct((rows, LANES), grads.dtype),
        scratch_shapes=[pltpu.VMEM((1, size), grads.dtype), pltpu.SemaphoreType.DMA((parts,))],
        compiler_params=pltpu.CompilerParams(vmem_limit_bytes=40 * MIB),
        cost_estimate=pl.CostEstimate(flops=0, bytes_accessed=6 * size, transcendentals=0),
    )(grads)


def fold(total):
    wide = total.shape[0]
    i = lax.broadcasted_iota(jnp.int32, (wide, wide), 0)
    j = lax.broadcasted_iota(jnp.int32, (wide, wide), 1)
    kept = jnp.where(i % PACK == j % PACK, total, 0.0)
    k = lax.broadcasted_iota(jnp.int32, (wide, LANES), 0)
    s = lax.broadcasted_iota(jnp.int32, (wide, LANES), 1)
    pick = jnp.where(k // PACK == s, 1.0, 0.0)
    columns = jnp.dot(kept, pick, precision=lax.Precision.HIGHEST, preferred_element_type=jnp.float32)
    return columns.reshape(wide // PACK, PACK, LANES).sum(axis=1)


def grid_of(rows):
    row = lax.broadcasted_iota(jnp.int32, (rows, LANES), 0)
    return row, lax.broadcasted_iota(jnp.int32, (rows, LANES), 1)


def distance_kernel(parts, x_ref, o_ref):
    count, rows, _ = x_ref.shape
    half = count // 2
    rows = rows // parts
    product = functools.partial(
        lax.dot_general, dimension_numbers=(((1,), (1,)), ((), ())), preferred_element_type=jnp.float32
    )

    def group(first, part):
        return jnp.concatenate(
            [
                x_ref[first : first + half, part * rows + j * PACK : part * rows + (j + 1) * PACK, :].reshape(
                    half * PACK, LANES
                )
                for j in range(rows // PACK)
            ],
            axis=1,
        )

    totals = None
    for part in range(parts):
        low, high = group(0, part), group(half, part)
        found = (product(low, low), product(high, low), product(high, high))
        totals = found if totals is None else tuple(a + b for a, b in zip(totals, found))
    low_low, high_low, high_high = (fold(t) for t in totals)
    i, s = grid_of(half)

    def squares(gram):
        own = jnp.where(i == s, gram, 0.0)
        return jnp.sum(own, axis=1, keepdims=True), jnp.sum(own, axis=0, keepdims=True)

    low_down, low_across = squares(low_low)
    high_down, high_across = squares(high_high)
    cross = high_down + low_across - 2.0 * high_low
    within_low = low_down + low_across - 2.0 * low_low
    within_high = high_down + high_across - 2.0 * high_high
    cross = jnp.where(s < half, cross, 0.0)
    within = jnp.where(s < i, within_low, jnp.where((s > i) & (s < half), within_high, 0.0))
    both = cross + pltpu.roll(within, half, 1)
    packed = both[:SHORT]
    for q in range(1, half // SHORT):
        packed = packed + pltpu.roll(both[SHORT * q : SHORT * (q + 1)], count * q, 1)
    o_ref[...] = packed


def partial_distances(blocks, parts):
    return pl.pallas_call(
        functools.partial(distance_kernel, parts),
        in_specs=[WHOLE],
        out_specs=WHOLE,
        out_shape=jax.ShapeDtypeStruct((SHORT, LANES), jnp.float32),
        compiler_params=pltpu.CompilerParams(vmem_limit_bytes=32 * MIB),
    )(blocks)


def all_distances(packed, count):
    half = count // 2
    i, s = grid_of(half)
    both = jnp.concatenate([packed] * (half // SHORT), axis=0)
    both = jnp.where(s // count == i // SHORT, both, 0.0)
    both = sum(pltpu.roll(both, count * q, 1) for q in range(1, half // SHORT)) + both
    turned = jnp.concatenate([both, jnp.zeros((LANES - half, LANES), jnp.float32)], axis=0).T
    cross, cross_turned = jnp.where(s < half, both, 0.0), turned[:half]
    within = jnp.where(s < half, pltpu.roll(both, LANES - half, 1), 0.0)
    within_turned = turned[half:count]
    low = jnp.where(s < i, within, jnp.where(s > i, within_turned, 0.0))
    high = jnp.where(s > i, within, jnp.where(s < i, within_turned, 0.0))
    return jnp.concatenate(
        [low + pltpu.roll(cross_turned, half, 1), cross + pltpu.roll(high, half, 1)], axis=0
    )


def weiszfeld(distances, total):
    count = distances.shape[0]
    r, t = grid_of(count)
    same = (t == r).astype(jnp.float32)
    weights = jnp.full((count, 1), 1.0 / count, jnp.float32)
    for _ in range(ITERS):
        across = jnp.sum(same * weights, axis=0, keepdims=True)
        query = jnp.sum(distances * across, axis=1, keepdims=True)
        spread = jnp.sum(weights * query, axis=0, keepdims=True)
        square = jnp.maximum((query - 0.5 * spread) / total, 0.0)
        inverse = 1.0 / jnp.sqrt(square + 1e-06)
        weights = inverse / jnp.sum(inverse, axis=0, keepdims=True)
    return weights, jnp.sum(same * weights, axis=0, keepdims=True)


def aggregate_kernel(total, d_ref, x_ref, o_ref, w_ref, coeffs):
    count, rows, _ = x_ref.shape
    weights, across = weiszfeld(all_distances(d_ref[...].sum(axis=0), count), total)
    w_ref[...] = across
    coeffs[...] = jnp.broadcast_to(weights.astype(jnp.bfloat16).astype(jnp.float32), (count, LANES))
    piece = 32

    @pl.loop(0, rows // piece)
    def _(k):
        at = pl.ds(pl.multiple_of(k * piece, piece), piece)
        sums = [None] * 4
        for r in range(count):
            term = x_ref[r, at, :].astype(jnp.float32) * coeffs[r : r + 1, :]
            sums[r % 4] = term if sums[r % 4] is None else sums[r % 4] + term
        o_ref[at, :] = ((sums[0] + sums[1]) + (sums[2] + sums[3])).astype(o_ref.dtype)


def aggregate_blocks(distances, blocks, total):
    count, rows, _ = blocks.shape
    return pl.pallas_call(
        functools.partial(aggregate_kernel, float(total)),
        in_specs=[WHOLE, WHOLE],
        out_specs=[WHOLE, WHOLE],
        out_shape=[
            jax.ShapeDtypeStruct((rows, LANES), blocks.dtype),
            jax.ShapeDtypeStruct((1, LANES), jnp.float32),
        ],
        scratch_shapes=[pltpu.VMEM((count, LANES), jnp.float32)],
        compiler_params=pltpu.CompilerParams(vmem_limit_bytes=32 * MIB),
    )(distances, blocks)


def send(array, first, second):
    pairs = []
    for y in range(SIDE):
        for z in range(SIDE):
            for core in range(CORES):
                dy, dz = (first, second) if core == 0 else (second, first)
                there = (y + dy) % SIDE * SIDE + (z + dz) % SIDE
                pairs.append(((y * SIDE + z) * CORES + core, there * CORES + core))
    return lax.ppermute(array, "rep", pairs)


def swap(array):
    return lax.ppermute(array, "rep", [(i, i ^ 1) for i in range(COUNT)])


def place_kernel(moves, rows, *refs):
    sources, (out, sems) = refs[: len(moves)], refs[-2:]
    me = lax.axis_index("rep")
    y, z, core = me // (SIDE * CORES), me // CORES % SIDE, me % CORES
    stores = []
    for source, pieces in zip(sources, moves):
        for at, first, second, swapped in pieces:
            owner = 1 - core if swapped else core
            dy = jnp.where(owner == 0, first, second)
            dz = jnp.where(owner == 0, second, first)
            block = ((y - dy + SIDE) % SIDE * SIDE + (z - dz + SIDE) % SIDE) * CORES + owner
            target = out.at[pl.ds(pl.multiple_of(block * rows, rows), rows)]
            stores.append(pltpu.make_async_copy(source.at[pl.ds(at, rows)], target, sems.at[len(stores)]))
    for store in stores:
        store.start()
    for store in stores:
        store.wait()


def place(out, rows, sources, moves):
    count = sum(len(m) for m in moves)
    args = list(sources) + ([] if out is None else [out])
    return pl.pallas_call(
        functools.partial(place_kernel, moves, rows),
        in_specs=[WHOLE] * len(sources) + ([] if out is None else [ANY]),
        out_specs=ANY,
        out_shape=jax.ShapeDtypeStruct((COUNT * rows, LANES), sources[0].dtype),
        scratch_shapes=[pltpu.SemaphoreType.DMA((count,))],
        input_output_aliases={} if out is None else {len(args) - 1: 0},
        compiler_params=pltpu.CompilerParams(vmem_limit_bytes=16 * MIB),
        cost_estimate=pl.CostEstimate(flops=0, bytes_accessed=count * rows * LANES * 2, transcendentals=0),
    )(*args)


def after(array, *others):
    return lax.optimization_barrier((array, *others))[0]


def gather(own):
    rows = own.shape[0]

    def moves(firsts, second, swapped):
        return [(k * rows, first, second, swapped) for k, first in enumerate(firsts)]

    up, low = (0, 1), (3, 2)
    one, three, two = send(own, 1, 0), send(own, 3, 0), send(own, 2, 0)
    upper = jnp.concatenate([own, one])
    lower = jnp.concatenate([three, two])
    upper_1, upper_3 = send(upper, 0, 1), send(upper, 0, 3)
    lower_1, lower_3 = send(lower, 0, 1), send(lower, 0, 3)
    upper_2, lower_2 = send(upper_1, 0, 1), send(lower_3, 0, 3)
    out = place(
        None,
        rows,
        [upper, lower, swap(upper), swap(lower)],
        [moves(up, 0, False), moves(low, 0, False), moves(up, 0, True), moves(low, 0, True)],
    )
    swapped = [swap(a) for a in (upper_1, upper_3, after(lower_1, out), after(lower_3, out))]
    layout = [(up, 1), (up, 3), (low, 1), (low, 3)]
    out = place(out, rows, [upper_1, upper_3, lower_1, lower_3], [moves(f, s, False) for f, s in layout])
    far = [swap(after(upper_2, out)), swap(after(lower_2, out))]
    out = place(
        out,
        rows,
        swapped + [upper_2, lower_2],
        [moves(f, s, True) for f, s in layout] + [moves(up, 2, False), moves(low, 2, False)],
    )
    return place(out, rows, far, [moves(up, 2, True), moves(low, 2, True)])


def body(grads):
    count = lax.axis_size("rep")
    total = grads.shape[1] * lax.axis_size("shard")
    slab = compact(grads, 8).reshape(count, -1, LANES)
    blocks = lax.all_to_all(slab, "rep", split_axis=0, concat_axis=0, tiled=True)
    part = partial_distances(blocks, 4)
    everyone = count * lax.axis_size("shard")
    distances = lax.all_to_all(
        jnp.broadcast_to(part[None], (everyone, SHORT, LANES)), ("rep", "shard"), 0, 0, tiled=True
    )
    local, weights = aggregate_blocks(distances, blocks, total)
    return (gather(local).reshape(-1), weights[0, :count])


def solution(mesh):
    placed = (P("rep", "shard"),)
    return jax.shard_map(
        body, mesh=mesh, in_specs=placed, out_specs=(P("shard"), P()), check_vma=False
    )
```

time: 184 us -> 175 us (0.951)
  waiting for transfers between devices: 18.1 us -> 11.9 us
  starting transfers between devices: 16 us -> 19.5 us
  blocking collectives: 125 us -> 122 us
  Pallas kernels: 23.1 us -> 20.4 us
    ppermute x9, waiting for transfers between devices: 18.1 us -> 11.9 us  [send(): return lax.ppermute(array, 'rep', pairs)]
    ppermute x8, starting transfers between devices: 6.48 us -> 10.5 us  [swap(): return lax.ppermute(array, 'rep', [(i, i ^ 1) for i in range(COUNT)])]
    all_to_all x1, blocking collectives: 19.8 us -> 17 us  [body(): lax.all_to_all(jnp.broadcast_to(part[None], (everyone, SHORT, LANES)), ('...]
    pallas_call x6, Pallas kernels: 16.9 us -> 14.4 us  [the longest x1 5.96 us: partial_distances(): pl.pallas_call(functools.partial(distance_kernel, parts), in_specs=[WHOLE...]
  transfers between devices with their start and end apart: 17 -> 17, of which waited for: 7 -> 5; matrix products, arithmetic and copies ran while one was open for 0% -> 0% of each run, Pallas kernels for 3% -> 3%
where the time goes in v3:
time: 175 us
  blocking collectives  122 us (70%)
  Pallas kernels  20.4 us (12%)
  starting transfers between devices  19.5 us (11%)
  waiting for transfers between devices  11.9 us (7%)
    all_to_all x1, blocking collectives, body(): lax.all_to_all(slab, 'rep', split_axis=0, concat_axis=0, tiled=True)  105 us
    all_to_all x1, blocking collectives, body(): lax.all_to_all(jnp.broadcast_to(part[None], (everyone, SHORT, LANES)), ('...  17 us
    ppermute x9, waiting for transfers between devices, send(): return lax.ppermute(array, 'rep', pairs)  11.9 us
    ppermute x8, starting transfers between devices, swap(): return lax.ppermute(array, 'rep', [(i, i ^ 1) for i in range(COUNT)])  10.5 us
    ppermute x9, starting transfers between devices, send(): return lax.ppermute(array, 'rep', pairs)  8.99 us
    pallas_call x1, Pallas kernels, compact(): pl.pallas_call(functools.partial(compact_kernel, parts, 512), in_specs=[A...  6.09 us
    pallas_call x1, Pallas kernels, partial_distances(): pl.pallas_call(functools.partial(distance_kernel, parts), in_specs=[WHOLE...  5.96 us
    pallas_call x4, Pallas kernels, place(): pl.pallas_call(functools.partial(place_kernel, moves, rows), in_specs=[WH...  5.6 us
  transfers between devices with their start and end apart: 17, of which 5 were waited for; matrix products, arithmetic and copies ran while one was open for 0% of the time, Pallas kernels for 3%

profile of v3, /device:TPU:1, one launch (start us, length us, event | category | flops | bytes accessed | tf_op | source)
XLA Modules:
  0.0 175.2 jit_solution(10715027736426889321)
XLA Ops:
  0.6 6.1 %shard_map.30 = bf16[32768,128]{1,0:T(8,128)(2,1)S(1)} custom-call(bf16[1,4194304]{1,0:T(2,128)(2,1)} %x_ref.1), custom_call_target="tpu_custom_call" | custom-call | bytes 25165824 | tf_op jit(solution)/shard_map/pallas_call | solution.py:44
  6.7 105.0 %all_to_all.10.x_ref = bf16[32,1024,128]{2,1,0:T(8,128)(2,1)S(1)} all-to-all(bf16[32,1024,128]{2,1,0:T(8,128)(2,1)S(1)} %bitcast.4), channel_id=1, replica_groups=mesh['rep'=32,'shard'=4] {'rep'}, dimensions={0} | all-to-all | bytes 16777216 | tf_op jit(solution)/shard_map/all_to_all | solution.py:280
  111.7 6.0 %shard_map.31 = f32[4,128]{1,0:T(4,128)S(1)} custom-call(bf16[32,1024,128]{2,1,0:T(8,128)(2,1)S(1)} %all_to_all.10.x_ref), custom_call_target="tpu_custom_call" | custom-call | tf_op jit(solution)/shard_map/pallas_call | solution.py:118
  117.7 17.0 %all_to_all.11.d_ref = f32[128,4,128]{2,1,0:T(4,128)S(1)} all-to-all(f32[128,4,128]{2,1,0:T(4,128)S(1)} %broadcast_in_dim.2), channel_id=1, replica_groups=mesh['rep'=32,'shard'=4] {'rep','shard'}, dimensions={0} | all-to-all | bytes 524288 | tf_op jit(solution)/shard_map/all_to_all | solution.py:283
  134.7 2.8 %shard_map.32 = (bf16[1024,128]{1,0:T(8,128)(2,1)S(1)}, f32[1,128]{1,0:T(1,128)S(1)}) custom-call(f32[128,4,128]{2,1,0:T(4,128)S(1)} %all_to_all.11.d_ref, bf16[32,1024,128]{2,1,0:T(8,128)(2,1)S(1)} %all_to_all.10.x_ref), custom_call_target="tpu_custom_call" | custom-call | tf_op jit(solution)/shard_map/pallas_call | solution.py:178
  137.5 0.1 collective-permute-start
  137.6 2.7 %collective-permute-start.4 = (bf16[1024,128]{1,0:T(8,128)(2,1)S(1)}, bf16[1024,128]{1,0:T(8,128)(2,1)S(1)}, u32[]{:S(2)}, u32[]{:S(2)}) collective-permute-start(bf16[1024,128]{1,0:T(8,128)(2,1)S(1)} %get-tuple-element.8), channel_id=1, source_target_pairs={{0,96},{4,28},{8,104},{12,4},{16,112},{20,12},{24,120},{28,20},{32... | collective-permute-start | bytes 786440 | tf_op jit(solution)/shard_map/ppermute | solution.py:199
  140.2 0.0 collective-permute-start.5
  140.2 4.0 %collective-permute-done = bf16[1024,128]{1,0:T(8,128)(2,1)S(1)} collective-permute-done((bf16[1024,128]{1,0:T(8,128)(2,1)S(1)}, bf16[1024,128]{1,0:T(8,128)(2,1)S(1)}, u32[]{:S(2)}, u32[]{:S(2)}) %collective-permute-start) | collective-permute-done | bytes 262176 | tf_op jit(solution)/shard_map/ppermute | solution.py:199
  144.3 1.2 collective-permute-start.8
  145.5 0.8 collective-permute-done.4
  146.4 0.9 collective-permute-done.5
  147.3 0.9 collective-permute-start.7
  148.2 0.6 collective-permute-start.1
  148.8 2.2 %collective-permute-start.9 = (bf16[2048,128]{1,0:T(8,128)(2,1)S(1)}, bf16[2048,128]{1,0:T(8,128)(2,1)S(1)}, u32[]{:S(2)}, u32[]{:S(2)}) collective-permute-start(bf16[2048,128]{1,0:T(8,128)(2,1)S(1)} %constant_dynamic-update-slice_fusion.2.refs_1_), channel_id=1, source_target_pairs={{0,4},{4,0},{8,12},{12,8},{16,20},{20,16},{24,28},{28,24},{32,36},... | collective-permute-start | bytes 1572872 | tf_op jit(solution)/shard_map/ppermute | solution.py:203
  151.1 0.0 collective-permute-start.6
  151.1 0.0 collective-permute-done.8.refs_2_
  151.1 2.7 %collective-permute-start.3 = (bf16[2048,128]{1,0:T(8,128)(2,1)S(1)}, bf16[2048,128]{1,0:T(8,128)(2,1)S(1)}, u32[]{:S(2)}, u32[]{:S(2)}) collective-permute-start(bf16[2048,128]{1,0:T(8,128)(2,1)S(1)} %constant_dynamic-update-slice_fusion.refs_0_), channel_id=1, source_target_pairs={{0,24},{4,100},{8,0},{12,108},{16,8},{20,116},{24,16},{28,124},{32... | collective-permute-start | bytes 1572872 | tf_op jit(solution)/shard_map/ppermute | solution.py:199
  153.7 1.9 %collective-permute-done.7.refs_3_ = bf16[2048,128]{1,0:T(8,128)(2,1)S(1)} collective-permute-done((bf16[2048,128]{1,0:T(8,128)(2,1)S(1)}, bf16[2048,128]{1,0:T(8,128)(2,1)S(1)}, u32[]{:S(2)}, u32[]{:S(2)}) %collective-permute-start.7) | collective-permute-done | bytes 524320 | tf_op jit(solution)/shard_map/ppermute | solution.py:199
  155.7 2.0 %collective-permute-start.11 = (bf16[2048,128]{1,0:T(8,128)(2,1)S(1)}, bf16[2048,128]{1,0:T(8,128)(2,1)S(1)}, u32[]{:S(2)}, u32[]{:S(2)}) collective-permute-start(bf16[2048,128]{1,0:T(8,128)(2,1)S(1)} %collective-permute-done.7.refs_3_), channel_id=1, source_target_pairs={{0,24},{4,100},{8,0},{12,108},{16,8},{20,116},{24,16},{28,124},{32... | collective-permute-start | bytes 1572872 | tf_op jit(solution)/shard_map/ppermute | solution.py:199
  157.7 1.4 shard_map.33.refs_4_
  159.1 4.2 %collective-permute-done.6.refs_2_ = bf16[2048,128]{1,0:T(8,128)(2,1)S(1)} collective-permute-done((bf16[2048,128]{1,0:T(8,128)(2,1)S(1)}, bf16[2048,128]{1,0:T(8,128)(2,1)S(1)}, u32[]{:S(2)}, u32[]{:S(2)}) %collective-permute-start.6) | collective-permute-done | bytes 524320 | tf_op jit(solution)/shard_map/ppermute | solution.py:199
  163.3 2.9 %collective-permute-start.15 = (bf16[2048,128]{1,0:T(8,128)(2,1)S(1)}, bf16[2048,128]{1,0:T(8,128)(2,1)S(1)}, u32[]{:S(2)}, u32[]{:S(2)}) collective-permute-start(bf16[2048,128]{1,0:T(8,128)(2,1)S(1)} %collective-permute-done.6.refs_2_), channel_id=1, source_target_pairs={{0,4},{4,0},{8,12},{12,8},{16,20},{20,16},{24,28},{28,24},{32,36},... | collective-permute-start | bytes 1572872 | tf_op jit(solution)/shard_map/ppermute | solution.py:203
  166.2 0.0 collective-permute-start.16
  166.2 0.5 collective-permute-start.13
  166.7 1.4 shard_map.34.refs_6_
  168.1 1.4 collective-permute-start.14
  169.5 2.4 %collective-permute-start.12 = (bf16[2048,128]{1,0:T(8,128)(2,1)S(1)}, bf16[2048,128]{1,0:T(8,128)(2,1)S(1)}, u32[]{:S(2)}, u32[]{:S(2)}) collective-permute-start(bf16[2048,128]{1,0:T(8,128)(2,1)S(1)} %collective-permute-done.11.refs_5_), channel_id=1, source_target_pairs={{0,4},{4,0},{8,12},{12,8},{16,20},{20,16},{24,28},{28,24},{32,36},... | collective-permute-start | bytes 1572872 | tf_op jit(solution)/shard_map/ppermute | solution.py:203
  171.8 0.0 collective-permute-start.10
  171.8 0.5 slice_bitcast_fusion
  172.3 1.8 %shard_map.35.refs_2_ = bf16[32768,128]{1,0:T(8,128)(2,1)} custom-call(bf16[2048,128]{1,0:T(8,128)(2,1)S(1)} %collective-permute-done.13.refs_0_, bf16[2048,128]{1,0:T(8,128)(2,1)S(1)} %collective-permute-done.14.refs_1_, bf16[2048,128]{1,0:T(8,128)(2,1)S(1)} %collective-permute-done.15.refs_2_, ...), custom_call_target="tpu_custom_call", output_to_operand_aliasing={{}: (6, {})} | custom-call | bytes 3145728 | tf_op jit(solution)/shard_map/pallas_call | solution.py:228
  174.2 1.0 shard_map.36
  (17 shorter events, 0.2 us)
Async XLA Ops:
  137.5 6.8 %collective-permute-start = (bf16[1024,128]{1,0:T(8,128)(2,1)S(1)}, bf16[1024,128]{1,0:T(8,128)(2,1)S(1)}, u32[]{:S(2)}, u32[]{:S(2)}) collective-permute-start(bf16[1024,128]{1,0:T(8,128)(2,1)S(1)} %get-tuple-element.8), channel_id=1, source_target_pairs={{0,32},{4,12},{8,40},{12,20},{16,48},{20,28},{24,56},{28,4},{32,64... | collective-permute-start | bytes 786440 | tf_op jit(solution)/shard_map/ppermute | solution.py:199
  137.6 8.8 %collective-permute-start.4 = (bf16[1024,128]{1,0:T(8,128)(2,1)S(1)}, bf16[1024,128]{1,0:T(8,128)(2,1)S(1)}, u32[]{:S(2)}, u32[]{:S(2)}) collective-permute-start(bf16[1024,128]{1,0:T(8,128)(2,1)S(1)} %get-tuple-element.8), channel_id=1, source_target_pairs={{0,96},{4,28},{8,104},{12,4},{16,112},{20,12},{24,120},{28,20},{32... | collective-permute-start | bytes 786440 | tf_op jit(solution)/shard_map/ppermute | solution.py:199
  140.2 7.0 %collective-permute-start.5 = (bf16[1024,128]{1,0:T(8,128)(2,1)S(1)}, bf16[1024,128]{1,0:T(8,128)(2,1)S(1)}, u32[]{:S(2)}, u32[]{:S(2)}) collective-permute-start(bf16[1024,128]{1,0:T(8,128)(2,1)S(1)} %get-tuple-element.8), channel_id=1, source_target_pairs={{0,64},{4,20},{8,72},{12,28},{16,80},{20,4},{24,88},{28,12},{32,96... | collective-permute-start | bytes 786440 | tf_op jit(solution)/shard_map/ppermute | solution.py:199
  144.3 6.8 %collective-permute-start.8 = (bf16[2048,128]{1,0:T(8,128)(2,1)S(1)}, bf16[2048,128]{1,0:T(8,128)(2,1)S(1)}, u32[]{:S(2)}, u32[]{:S(2)}) collective-permute-start(bf16[2048,128]{1,0:T(8,128)(2,1)S(1)} %constant_dynamic-update-slice_fusion.refs_0_), channel_id=1, source_target_pairs={{0,4},{4,0},{8,12},{12,8},{16,20},{20,16},{24,28},{28,24},{32,36},... | collective-permute-start | bytes 1572872 | tf_op jit(solution)/shard_map/ppermute | solution.py:203
  147.3 8.4 %collective-permute-start.7 = (bf16[2048,128]{1,0:T(8,128)(2,1)S(1)}, bf16[2048,128]{1,0:T(8,128)(2,1)S(1)}, u32[]{:S(2)}, u32[]{:S(2)}) collective-permute-start(bf16[2048,128]{1,0:T(8,128)(2,1)S(1)} %constant_dynamic-update-slice_fusion.2.refs_1_), channel_id=1, source_target_pairs={{0,24},{4,100},{8,0},{12,108},{16,8},{20,116},{24,16},{28,124},{32... | collective-permute-start | bytes 1572872 | tf_op jit(solution)/shard_map/ppermute | solution.py:199
  148.2 9.5 %collective-permute-start.1 = (bf16[2048,128]{1,0:T(8,128)(2,1)S(1)}, bf16[2048,128]{1,0:T(8,128)(2,1)S(1)}, u32[]{:S(2)}, u32[]{:S(2)}) collective-permute-start(bf16[2048,128]{1,0:T(8,128)(2,1)S(1)} %constant_dynamic-update-slice_fusion.refs_0_), channel_id=1, source_target_pairs={{0,8},{4,36},{8,16},{12,44},{16,24},{20,52},{24,0},{28,60},{32,40}... | collective-permute-start | bytes 1572872 | tf_op jit(solution)/shard_map/ppermute | solution.py:199
  148.8 8.9 %collective-permute-start.9 = (bf16[2048,128]{1,0:T(8,128)(2,1)S(1)}, bf16[2048,128]{1,0:T(8,128)(2,1)S(1)}, u32[]{:S(2)}, u32[]{:S(2)}) collective-permute-start(bf16[2048,128]{1,0:T(8,128)(2,1)S(1)} %constant_dynamic-update-slice_fusion.2.refs_1_), channel_id=1, source_target_pairs={{0,4},{4,0},{8,12},{12,8},{16,20},{20,16},{24,28},{28,24},{32,36},... | collective-permute-start | bytes 1572872 | tf_op jit(solution)/shard_map/ppermute | solution.py:203
  151.1 12.3 %collective-permute-start.6 = (bf16[2048,128]{1,0:T(8,128)(2,1)S(1)}, bf16[2048,128]{1,0:T(8,128)(2,1)S(1)}, u32[]{:S(2)}, u32[]{:S(2)}) collective-permute-start(bf16[2048,128]{1,0:T(8,128)(2,1)S(1)} %constant_dynamic-update-slice_fusion.2.refs_1_), channel_id=1, source_target_pairs={{0,8},{4,36},{8,16},{12,44},{16,24},{20,52},{24,0},{28,60},{32,40}... | collective-permute-start | bytes 1572872 | tf_op jit(solution)/shard_map/ppermute | solution.py:199
  151.1 15.1 %collective-permute-start.3 = (bf16[2048,128]{1,0:T(8,128)(2,1)S(1)}, bf16[2048,128]{1,0:T(8,128)(2,1)S(1)}, u32[]{:S(2)}, u32[]{:S(2)}) collective-permute-start(bf16[2048,128]{1,0:T(8,128)(2,1)S(1)} %constant_dynamic-update-slice_fusion.refs_0_), channel_id=1, source_target_pairs={{0,24},{4,100},{8,0},{12,108},{16,8},{20,116},{24,16},{28,124},{32... | collective-permute-start | bytes 1572872 | tf_op jit(solution)/shard_map/ppermute | solution.py:199
  155.7 12.4 %collective-permute-start.11 = (bf16[2048,128]{1,0:T(8,128)(2,1)S(1)}, bf16[2048,128]{1,0:T(8,128)(2,1)S(1)}, u32[]{:S(2)}, u32[]{:S(2)}) collective-permute-start(bf16[2048,128]{1,0:T(8,128)(2,1)S(1)} %collective-permute-done.7.refs_3_), channel_id=1, source_target_pairs={{0,24},{4,100},{8,0},{12,108},{16,8},{20,116},{24,16},{28,124},{32... | collective-permute-start | bytes 1572872 | tf_op jit(solution)/shard_map/ppermute | solution.py:199
  157.7 11.7 %collective-permute-start.2 = (bf16[2048,128]{1,0:T(8,128)(2,1)S(1)}, bf16[2048,128]{1,0:T(8,128)(2,1)S(1)}, u32[]{:S(2)}, u32[]{:S(2)}) collective-permute-start(bf16[2048,128]{1,0:T(8,128)(2,1)S(1)} %collective-permute-done.1.refs_0_), channel_id=1, source_target_pairs={{0,8},{4,36},{8,16},{12,44},{16,24},{20,52},{24,0},{28,60},{32,40}... | collective-permute-start | bytes 1572872 | tf_op jit(solution)/shard_map/ppermute | solution.py:199
  163.3 8.5 %collective-permute-start.15 = (bf16[2048,128]{1,0:T(8,128)(2,1)S(1)}, bf16[2048,128]{1,0:T(8,128)(2,1)S(1)}, u32[]{:S(2)}, u32[]{:S(2)}) collective-permute-start(bf16[2048,128]{1,0:T(8,128)(2,1)S(1)} %collective-permute-done.6.refs_2_), channel_id=1, source_target_pairs={{0,4},{4,0},{8,12},{12,8},{16,20},{20,16},{24,28},{28,24},{32,36},... | collective-permute-start | bytes 1572872 | tf_op jit(solution)/shard_map/ppermute | solution.py:203
  166.2 6.1 %collective-permute-start.16 = (bf16[2048,128]{1,0:T(8,128)(2,1)S(1)}, bf16[2048,128]{1,0:T(8,128)(2,1)S(1)}, u32[]{:S(2)}, u32[]{:S(2)}) collective-permute-start(bf16[2048,128]{1,0:T(8,128)(2,1)S(1)} %collective-permute-done.7.refs_3_), channel_id=1, source_target_pairs={{0,4},{4,0},{8,12},{12,8},{16,20},{20,16},{24,28},{28,24},{32,36},... | collective-permute-start | bytes 1572872 | tf_op jit(solution)/shard_map/ppermute | solution.py:203
  166.2 6.1 %collective-permute-start.13 = (bf16[2048,128]{1,0:T(8,128)(2,1)S(1)}, bf16[2048,128]{1,0:T(8,128)(2,1)S(1)}, u32[]{:S(2)}, u32[]{:S(2)}) collective-permute-start(bf16[2048,128]{1,0:T(8,128)(2,1)S(1)} %collective-permute-done.1.refs_0_), channel_id=1, source_target_pairs={{0,4},{4,0},{8,12},{12,8},{16,20},{20,16},{24,28},{28,24},{32,36},... | collective-permute-start | bytes 1572872 | tf_op jit(solution)/shard_map/ppermute | solution.py:203
  168.1 4.2 %collective-permute-start.14 = (bf16[2048,128]{1,0:T(8,128)(2,1)S(1)}, bf16[2048,128]{1,0:T(8,128)(2,1)S(1)}, u32[]{:S(2)}, u32[]{:S(2)}) collective-permute-start(bf16[2048,128]{1,0:T(8,128)(2,1)S(1)} %collective-permute-done.3.refs_1_), channel_id=1, source_target_pairs={{0,4},{4,0},{8,12},{12,8},{16,20},{20,16},{24,28},{28,24},{32,36},... | collective-permute-start | bytes 1572872 | tf_op jit(solution)/shard_map/ppermute | solution.py:203
  169.5 4.7 %collective-permute-start.12 = (bf16[2048,128]{1,0:T(8,128)(2,1)S(1)}, bf16[2048,128]{1,0:T(8,128)(2,1)S(1)}, u32[]{:S(2)}, u32[]{:S(2)}) collective-permute-start(bf16[2048,128]{1,0:T(8,128)(2,1)S(1)} %collective-permute-done.11.refs_5_), channel_id=1, source_target_pairs={{0,4},{4,0},{8,12},{12,8},{16,20},{20,16},{24,28},{28,24},{32,36},... | collective-permute-start | bytes 1572872 | tf_op jit(solution)/shard_map/ppermute | solution.py:203
  171.8 2.3 %collective-permute-start.10 = (bf16[2048,128]{1,0:T(8,128)(2,1)S(1)}, bf16[2048,128]{1,0:T(8,128)(2,1)S(1)}, u32[]{:S(2)}, u32[]{:S(2)}) collective-permute-start(bf16[2048,128]{1,0:T(8,128)(2,1)S(1)} %collective-permute-done.2.refs_4_), channel_id=1, source_target_pairs={{0,4},{4,0},{8,12},{12,8},{16,20},{20,16},{24,28},{28,24},{32,36},... | collective-permute-start | bytes 1572872 | tf_op jit(solution)/shard_map/ppermute | solution.py:203

commit v4 on v3

--- a/solution.py
+++ b/solution.py
@@ -241,7 +241,7 @@
     return lax.optimization_barrier((array, *others))[0]
 
 
-def gather(own):
+def gather(own, *early):
     rows = own.shape[0]
 
     def moves(firsts, second, swapped):
@@ -253,14 +253,14 @@
     lower = jnp.concatenate([three, two])
     upper_1, upper_3 = send(upper, 0, 1), send(upper, 0, 3)
     lower_1, lower_3 = send(lower, 0, 1), send(lower, 0, 3)
-    upper_2, lower_2 = send(upper_1, 0, 1), send(lower_3, 0, 3)
+    upper_2, lower_2 = send(upper_3, 0, 3), send(lower_1, 0, 1)
     out = place(
         None,
         rows,
         [upper, lower, swap(upper), swap(lower)],
         [moves(up, 0, False), moves(low, 0, False), moves(up, 0, True), moves(low, 0, True)],
     )
-    swapped = [swap(a) for a in (upper_1, upper_3, after(lower_1, out), after(lower_3, out))]
+    swapped = [swap(a) for a in (upper_1, upper_3, after(lower_1, out, *early), after(lower_3, out))]
     layout = [(up, 1), (up, 3), (low, 1), (low, 3)]
     out = place(out, rows, [upper_1, upper_3, lower_1, lower_3], [moves(f, s, False) for f, s in layout])
     far = [swap(after(upper_2, out)), swap(after(lower_2, out))]
@@ -278,13 +278,14 @@
     total = grads.shape[1] * lax.axis_size("shard")
     slab = compact(grads, 8).reshape(count, -1, LANES)
     blocks = lax.all_to_all(slab, "rep", split_axis=0, concat_axis=0, tiled=True)
-    part = partial_distances(blocks, 4)
+    part = partial_distances(blocks, 1)
     everyone = count * lax.axis_size("shard")
     distances = lax.all_to_all(
         jnp.broadcast_to(part[None], (everyone, SHORT, LANES)), ("rep", "shard"), 0, 0, tiled=True
     )
     local, weights = aggregate_blocks(distances, blocks, total)
-    return (gather(local).reshape(-1), weights[0, :count])
+    weights = weights[0, :count]
+    return (gather(local, weights).reshape(-1), weights)
 
 
 def solution(mesh):

time: 175 us -> 175 us (level)
    ppermute x8, starting transfers between devices: 10.5 us -> 8.59 us  [swap(): return lax.ppermute(array, 'rep', [(i, i ^ 1) for i in range(COUNT)])]
  transfers between devices with their start and end apart: 17 -> 17, of which waited for: 5 -> 6; matrix products, arithmetic and copies ran while one was open for 0% -> 0% of each run, Pallas kernels for 3% -> 3%
where the time goes in v4:
time: 175 us; the launch traced here: 174 us
  blocking collectives  122 us (70%)
  Pallas kernels  19.8 us (11%)
  starting transfers between devices  19 us (11%)
  waiting for transfers between devices  12.3 us (7%)
    all_to_all x1, blocking collectives, body(): lax.all_to_all(slab, 'rep', split_axis=0, concat_axis=0, tiled=True)  105 us
    all_to_all x1, blocking collectives, body(): lax.all_to_all(jnp.broadcast_to(part[None], (everyone, SHORT, LANES)), ('...  17 us
    ppermute x9, waiting for transfers between devices, send(): return lax.ppermute(array, 'rep', pairs)  11.2 us
    ppermute x9, starting transfers between devices, send(): return lax.ppermute(array, 'rep', pairs)  10.4 us
    ppermute x8, starting transfers between devices, swap(): return lax.ppermute(array, 'rep', [(i, i ^ 1) for i in range(COUNT)])  8.59 us
    pallas_call x1, Pallas kernels, compact(): pl.pallas_call(functools.partial(compact_kernel, parts, 512), in_specs=[A...  6.09 us
    pallas_call x4, Pallas kernels, place(): pl.pallas_call(functools.partial(place_kernel, moves, rows), in_specs=[WH...  5.53 us
    pallas_call x1, Pallas kernels, partial_distances(): pl.pallas_call(functools.partial(distance_kernel, parts), in_specs=[WHOLE...  5.36 us
  transfers between devices with their start and end apart: 17, of which 6 were waited for; matrix products, arithmetic and copies ran while one was open for 0% of the time, Pallas kernels for 3%

profile of v4, /device:TPU:1, one launch (start us, length us, event | category | flops | bytes accessed | tf_op | source)
XLA Modules:
  0.0 174.4 jit_solution(3631795796205086834)
XLA Ops:
  0.6 6.1 %shard_map.30 = bf16[32768,128]{1,0:T(8,128)(2,1)S(1)} custom-call(bf16[1,4194304]{1,0:T(2,128)(2,1)} %x_ref.1), custom_call_target="tpu_custom_call" | custom-call | bytes 25165824 | tf_op jit(solution)/shard_map/pallas_call | solution.py:44
  6.7 105.0 %all_to_all.10.x_ref = bf16[32,1024,128]{2,1,0:T(8,128)(2,1)S(1)} all-to-all(bf16[32,1024,128]{2,1,0:T(8,128)(2,1)S(1)} %bitcast.4), channel_id=1, replica_groups=mesh['rep'=32,'shard'=4] {'rep'}, dimensions={0} | all-to-all | bytes 16777216 | tf_op jit(solution)/shard_map/all_to_all | solution.py:280
  111.7 5.4 %shard_map.31 = f32[4,128]{1,0:T(4,128)S(1)} custom-call(bf16[32,1024,128]{2,1,0:T(8,128)(2,1)S(1)} %all_to_all.10.x_ref), custom_call_target="tpu_custom_call" | custom-call | tf_op jit(solution)/shard_map/pallas_call | solution.py:118
  117.1 17.0 %all_to_all.11.d_ref = f32[128,4,128]{2,1,0:T(4,128)S(1)} all-to-all(f32[128,4,128]{2,1,0:T(4,128)S(1)} %broadcast_in_dim.2), channel_id=1, replica_groups=mesh['rep'=32,'shard'=4] {'rep','shard'}, dimensions={0} | all-to-all | bytes 524288 | tf_op jit(solution)/shard_map/all_to_all | solution.py:283
  134.1 2.8 %shard_map.32 = (bf16[1024,128]{1,0:T(8,128)(2,1)S(1)}, f32[1,128]{1,0:T(1,128)S(1)}) custom-call(f32[128,4,128]{2,1,0:T(4,128)S(1)} %all_to_all.11.d_ref, bf16[32,1024,128]{2,1,0:T(8,128)(2,1)S(1)} %all_to_all.10.x_ref), custom_call_target="tpu_custom_call" | custom-call | tf_op jit(solution)/shard_map/pallas_call | solution.py:178
  136.9 0.1 collective-permute-start
  137.0 2.7 %collective-permute-start.4 = (bf16[1024,128]{1,0:T(8,128)(2,1)S(1)}, bf16[1024,128]{1,0:T(8,128)(2,1)S(1)}, u32[]{:S(2)}, u32[]{:S(2)}) collective-permute-start(bf16[1024,128]{1,0:T(8,128)(2,1)S(1)} %get-tuple-element.8), channel_id=1, source_target_pairs={{0,96},{4,28},{8,104},{12,4},{16,112},{20,12},{24,120},{28,20},{32... | collective-permute-start | bytes 786440 | tf_op jit(solution)/shard_map/ppermute | solution.py:199
  139.6 0.0 collective-permute-start.5
  139.6 4.0 %collective-permute-done = bf16[1024,128]{1,0:T(8,128)(2,1)S(1)} collective-permute-done((bf16[1024,128]{1,0:T(8,128)(2,1)S(1)}, bf16[1024,128]{1,0:T(8,128)(2,1)S(1)}, u32[]{:S(2)}, u32[]{:S(2)}) %collective-permute-start) | collective-permute-done | bytes 262176 | tf_op jit(solution)/shard_map/ppermute | solution.py:199
  143.7 1.2 collective-permute-start.8
  144.9 0.8 collective-permute-done.4
  145.8 0.9 collective-permute-done.5
  146.7 0.1 collective-permute-start.6
  146.8 2.6 %collective-permute-start.1 = (bf16[2048,128]{1,0:T(8,128)(2,1)S(1)}, bf16[2048,128]{1,0:T(8,128)(2,1)S(1)}, u32[]{:S(2)}, u32[]{:S(2)}) collective-permute-start(bf16[2048,128]{1,0:T(8,128)(2,1)S(1)} %constant_dynamic-update-slice_fusion.refs_0_), channel_id=1, source_target_pairs={{0,24},{4,100},{8,0},{12,108},{16,8},{20,116},{24,16},{28,124},{32... | collective-permute-start | bytes 1572872 | tf_op jit(solution)/shard_map/ppermute | solution.py:199
  149.4 2.2 %collective-permute-start.9 = (bf16[2048,128]{1,0:T(8,128)(2,1)S(1)}, bf16[2048,128]{1,0:T(8,128)(2,1)S(1)}, u32[]{:S(2)}, u32[]{:S(2)}) collective-permute-start(bf16[2048,128]{1,0:T(8,128)(2,1)S(1)} %constant_dynamic-update-slice_fusion.2.refs_1_), channel_id=1, source_target_pairs={{0,4},{4,0},{8,12},{12,8},{16,20},{20,16},{24,28},{28,24},{32,36},... | collective-permute-start | bytes 1572872 | tf_op jit(solution)/shard_map/ppermute | solution.py:203
  151.7 2.3 %collective-permute-start.7 = (bf16[2048,128]{1,0:T(8,128)(2,1)S(1)}, bf16[2048,128]{1,0:T(8,128)(2,1)S(1)}, u32[]{:S(2)}, u32[]{:S(2)}) collective-permute-start(bf16[2048,128]{1,0:T(8,128)(2,1)S(1)} %constant_dynamic-update-slice_fusion.2.refs_1_), channel_id=1, source_target_pairs={{0,24},{4,100},{8,0},{12,108},{16,8},{20,116},{24,16},{28,124},{32... | collective-permute-start | bytes 1572872 | tf_op jit(solution)/shard_map/ppermute | solution.py:199
  154.0 2.3 %collective-permute-done.6.refs_2_ = bf16[2048,128]{1,0:T(8,128)(2,1)S(1)} collective-permute-done((bf16[2048,128]{1,0:T(8,128)(2,1)S(1)}, bf16[2048,128]{1,0:T(8,128)(2,1)S(1)}, u32[]{:S(2)}, u32[]{:S(2)}) %collective-permute-start.6) | collective-permute-done | bytes 524320 | tf_op jit(solution)/shard_map/ppermute | solution.py:199
  156.3 0.5 slice_bitcast_fusion
  156.8 0.0 collective-permute-done.1.refs_1_
  156.8 2.7 %collective-permute-start.2 = (bf16[2048,128]{1,0:T(8,128)(2,1)S(1)}, bf16[2048,128]{1,0:T(8,128)(2,1)S(1)}, u32[]{:S(2)}, u32[]{:S(2)}) collective-permute-start(bf16[2048,128]{1,0:T(8,128)(2,1)S(1)} %collective-permute-done.1.refs_1_), channel_id=1, source_target_pairs={{0,24},{4,100},{8,0},{12,108},{16,8},{20,116},{24,16},{28,124},{32... | collective-permute-start | bytes 1572872 | tf_op jit(solution)/shard_map/ppermute | solution.py:199
  159.5 1.4 shard_map.33.refs_4_
  160.9 3.2 %collective-permute-start.15 = (bf16[2048,128]{1,0:T(8,128)(2,1)S(1)}, bf16[2048,128]{1,0:T(8,128)(2,1)S(1)}, u32[]{:S(2)}, u32[]{:S(2)}) collective-permute-start(bf16[2048,128]{1,0:T(8,128)(2,1)S(1)} %collective-permute-done.6.refs_2_), channel_id=1, source_target_pairs={{0,4},{4,0},{8,12},{12,8},{16,20},{20,16},{24,28},{28,24},{32,36},... | collective-permute-start | bytes 1572872 | tf_op jit(solution)/shard_map/ppermute | solution.py:203
  164.0 0.1 collective-permute-start.16
  164.2 0.4 collective-permute-start.14
  164.6 1.4 shard_map.34.refs_6_
  165.9 3.2 %collective-permute-done.11.refs_5_ = bf16[2048,128]{1,0:T(8,128)(2,1)S(1)} collective-permute-done((bf16[2048,128]{1,0:T(8,128)(2,1)S(1)}, bf16[2048,128]{1,0:T(8,128)(2,1)S(1)}, u32[]{:S(2)}, u32[]{:S(2)}) %collective-permute-start.11) | collective-permute-done | bytes 524320 | tf_op jit(solution)/shard_map/ppermute | solution.py:199
  169.1 1.0 collective-permute-start.13
  170.1 0.0 collective-permute-start.12
  170.1 0.5 collective-permute-start.10
  170.6 1.0 collective-permute-done.13.refs_0_
  171.6 1.8 %shard_map.35.refs_2_ = bf16[32768,128]{1,0:T(8,128)(2,1)} custom-call(bf16[2048,128]{1,0:T(8,128)(2,1)S(1)} %collective-permute-done.13.refs_0_, bf16[2048,128]{1,0:T(8,128)(2,1)S(1)} %collective-permute-done.14.refs_1_, bf16[2048,128]{1,0:T(8,128)(2,1)S(1)} %collective-permute-done.15.refs_2_, ...), custom_call_target="tpu_custom_call", output_to_operand_aliasing={{}: (6, {})} | custom-call | bytes 3145728 | tf_op jit(solution)/shard_map/pallas_call | solution.py:228
  173.4 1.0 shard_map.36
  (17 shorter events, 0.2 us)
Async XLA Ops:
  136.9 6.8 %collective-permute-start = (bf16[1024,128]{1,0:T(8,128)(2,1)S(1)}, bf16[1024,128]{1,0:T(8,128)(2,1)S(1)}, u32[]{:S(2)}, u32[]{:S(2)}) collective-permute-start(bf16[1024,128]{1,0:T(8,128)(2,1)S(1)} %get-tuple-element.8), channel_id=1, source_target_pairs={{0,32},{4,12},{8,40},{12,20},{16,48},{20,28},{24,56},{28,4},{32,64... | collective-permute-start | bytes 786440 | tf_op jit(solution)/shard_map/ppermute | solution.py:199
  137.0 8.8 %collective-permute-start.4 = (bf16[1024,128]{1,0:T(8,128)(2,1)S(1)}, bf16[1024,128]{1,0:T(8,128)(2,1)S(1)}, u32[]{:S(2)}, u32[]{:S(2)}) collective-permute-start(bf16[1024,128]{1,0:T(8,128)(2,1)S(1)} %get-tuple-element.8), channel_id=1, source_target_pairs={{0,96},{4,28},{8,104},{12,4},{16,112},{20,12},{24,120},{28,20},{32... | collective-permute-start | bytes 786440 | tf_op jit(solution)/shard_map/ppermute | solution.py:199
  139.6 7.0 %collective-permute-start.5 = (bf16[1024,128]{1,0:T(8,128)(2,1)S(1)}, bf16[1024,128]{1,0:T(8,128)(2,1)S(1)}, u32[]{:S(2)}, u32[]{:S(2)}) collective-permute-start(bf16[1024,128]{1,0:T(8,128)(2,1)S(1)} %get-tuple-element.8), channel_id=1, source_target_pairs={{0,64},{4,20},{8,72},{12,28},{16,80},{20,4},{24,88},{28,12},{32,96... | collective-permute-start | bytes 786440 | tf_op jit(solution)/shard_map/ppermute | solution.py:199
  143.7 10.2 %collective-permute-start.8 = (bf16[2048,128]{1,0:T(8,128)(2,1)S(1)}, bf16[2048,128]{1,0:T(8,128)(2,1)S(1)}, u32[]{:S(2)}, u32[]{:S(2)}) collective-permute-start(bf16[2048,128]{1,0:T(8,128)(2,1)S(1)} %constant_dynamic-update-slice_fusion.refs_0_), channel_id=1, source_target_pairs={{0,4},{4,0},{8,12},{12,8},{16,20},{20,16},{24,28},{28,24},{32,36},... | collective-permute-start | bytes 1572872 | tf_op jit(solution)/shard_map/ppermute | solution.py:203
  146.7 9.6 %collective-permute-start.6 = (bf16[2048,128]{1,0:T(8,128)(2,1)S(1)}, bf16[2048,128]{1,0:T(8,128)(2,1)S(1)}, u32[]{:S(2)}, u32[]{:S(2)}) collective-permute-start(bf16[2048,128]{1,0:T(8,128)(2,1)S(1)} %constant_dynamic-update-slice_fusion.2.refs_1_), channel_id=1, source_target_pairs={{0,8},{4,36},{8,16},{12,44},{16,24},{20,52},{24,0},{28,60},{32,40}... | collective-permute-start | bytes 1572872 | tf_op jit(solution)/shard_map/ppermute | solution.py:199
  146.8 10.0 %collective-permute-start.1 = (bf16[2048,128]{1,0:T(8,128)(2,1)S(1)}, bf16[2048,128]{1,0:T(8,128)(2,1)S(1)}, u32[]{:S(2)}, u32[]{:S(2)}) collective-permute-start(bf16[2048,128]{1,0:T(8,128)(2,1)S(1)} %constant_dynamic-update-slice_fusion.refs_0_), channel_id=1, source_target_pairs={{0,24},{4,100},{8,0},{12,108},{16,8},{20,116},{24,16},{28,124},{32... | collective-permute-start | bytes 1572872 | tf_op jit(solution)/shard_map/ppermute | solution.py:199
  149.4 10.1 %collective-permute-start.9 = (bf16[2048,128]{1,0:T(8,128)(2,1)S(1)}, bf16[2048,128]{1,0:T(8,128)(2,1)S(1)}, u32[]{:S(2)}, u32[]{:S(2)}) collective-permute-start(bf16[2048,128]{1,0:T(8,128)(2,1)S(1)} %constant_dynamic-update-slice_fusion.2.refs_1_), channel_id=1, source_target_pairs={{0,4},{4,0},{8,12},{12,8},{16,20},{20,16},{24,28},{28,24},{32,36},... | collective-permute-start | bytes 1572872 | tf_op jit(solution)/shard_map/ppermute | solution.py:203
  151.7 12.4 %collective-permute-start.7 = (bf16[2048,128]{1,0:T(8,128)(2,1)S(1)}, bf16[2048,128]{1,0:T(8,128)(2,1)S(1)}, u32[]{:S(2)}, u32[]{:S(2)}) collective-permute-start(bf16[2048,128]{1,0:T(8,128)(2,1)S(1)} %constant_dynamic-update-slice_fusion.2.refs_1_), channel_id=1, source_target_pairs={{0,24},{4,100},{8,0},{12,108},{16,8},{20,116},{24,16},{28,124},{32... | collective-permute-start | bytes 1572872 | tf_op jit(solution)/shard_map/ppermute | solution.py:199
  153.9 10.2 %collective-permute-start.3 = (bf16[2048,128]{1,0:T(8,128)(2,1)S(1)}, bf16[2048,128]{1,0:T(8,128)(2,1)S(1)}, u32[]{:S(2)}, u32[]{:S(2)}) collective-permute-start(bf16[2048,128]{1,0:T(8,128)(2,1)S(1)} %constant_dynamic-update-slice_fusion.refs_0_), channel_id=1, source_target_pairs={{0,8},{4,36},{8,16},{12,44},{16,24},{20,52},{24,0},{28,60},{32,40}... | collective-permute-start | bytes 1572872 | tf_op jit(solution)/shard_map/ppermute | solution.py:199
  156.3 12.8 %collective-permute-start.11 = (bf16[2048,128]{1,0:T(8,128)(2,1)S(1)}, bf16[2048,128]{1,0:T(8,128)(2,1)S(1)}, u32[]{:S(2)}, u32[]{:S(2)}) collective-permute-start(bf16[2048,128]{1,0:T(8,128)(2,1)S(1)} %collective-permute-done.6.refs_2_), channel_id=1, source_target_pairs={{0,8},{4,36},{8,16},{12,44},{16,24},{20,52},{24,0},{28,60},{32,40}... | collective-permute-start | bytes 1572872 | tf_op jit(solution)/shard_map/ppermute | solution.py:199
  156.8 13.3 %collective-permute-start.2 = (bf16[2048,128]{1,0:T(8,128)(2,1)S(1)}, bf16[2048,128]{1,0:T(8,128)(2,1)S(1)}, u32[]{:S(2)}, u32[]{:S(2)}) collective-permute-start(bf16[2048,128]{1,0:T(8,128)(2,1)S(1)} %collective-permute-done.1.refs_1_), channel_id=1, source_target_pairs={{0,24},{4,100},{8,0},{12,108},{16,8},{20,116},{24,16},{28,124},{32... | collective-permute-start | bytes 1572872 | tf_op jit(solution)/shard_map/ppermute | solution.py:199
  160.9 9.2 %collective-permute-start.15 = (bf16[2048,128]{1,0:T(8,128)(2,1)S(1)}, bf16[2048,128]{1,0:T(8,128)(2,1)S(1)}, u32[]{:S(2)}, u32[]{:S(2)}) collective-permute-start(bf16[2048,128]{1,0:T(8,128)(2,1)S(1)} %collective-permute-done.6.refs_2_), channel_id=1, source_target_pairs={{0,4},{4,0},{8,12},{12,8},{16,20},{20,16},{24,28},{28,24},{32,36},... | collective-permute-start | bytes 1572872 | tf_op jit(solution)/shard_map/ppermute | solution.py:203
  164.0 6.5 %collective-permute-start.16 = (bf16[2048,128]{1,0:T(8,128)(2,1)S(1)}, bf16[2048,128]{1,0:T(8,128)(2,1)S(1)}, u32[]{:S(2)}, u32[]{:S(2)}) collective-permute-start(bf16[2048,128]{1,0:T(8,128)(2,1)S(1)} %collective-permute-done.7.refs_3_), channel_id=1, source_target_pairs={{0,4},{4,0},{8,12},{12,8},{16,20},{20,16},{24,28},{28,24},{32,36},... | collective-permute-start | bytes 1572872 | tf_op jit(solution)/shard_map/ppermute | solution.py:203
  164.2 6.4 %collective-permute-start.14 = (bf16[2048,128]{1,0:T(8,128)(2,1)S(1)}, bf16[2048,128]{1,0:T(8,128)(2,1)S(1)}, u32[]{:S(2)}, u32[]{:S(2)}) collective-permute-start(bf16[2048,128]{1,0:T(8,128)(2,1)S(1)} %collective-permute-done.1.refs_1_), channel_id=1, source_target_pairs={{0,4},{4,0},{8,12},{12,8},{16,20},{20,16},{24,28},{28,24},{32,36},... | collective-permute-start | bytes 1572872 | tf_op jit(solution)/shard_map/ppermute | solution.py:203
  169.1 2.5 %collective-permute-start.13 = (bf16[2048,128]{1,0:T(8,128)(2,1)S(1)}, bf16[2048,128]{1,0:T(8,128)(2,1)S(1)}, u32[]{:S(2)}, u32[]{:S(2)}) collective-permute-start(bf16[2048,128]{1,0:T(8,128)(2,1)S(1)} %collective-permute-done.3.refs_0_), channel_id=1, source_target_pairs={{0,4},{4,0},{8,12},{12,8},{16,20},{20,16},{24,28},{28,24},{32,36},... | collective-permute-start | bytes 1572872 | tf_op jit(solution)/shard_map/ppermute | solution.py:203
  170.1 3.3 %collective-permute-start.12 = (bf16[2048,128]{1,0:T(8,128)(2,1)S(1)}, bf16[2048,128]{1,0:T(8,128)(2,1)S(1)}, u32[]{:S(2)}, u32[]{:S(2)}) collective-permute-start(bf16[2048,128]{1,0:T(8,128)(2,1)S(1)} %collective-permute-done.11.refs_5_), channel_id=1, source_target_pairs={{0,4},{4,0},{8,12},{12,8},{16,20},{20,16},{24,28},{28,24},{32,36},... | collective-permute-start | bytes 1572872 | tf_op jit(solution)/shard_map/ppermute | solution.py:203
  170.1 3.3 %collective-permute-start.10 = (bf16[2048,128]{1,0:T(8,128)(2,1)S(1)}, bf16[2048,128]{1,0:T(8,128)(2,1)S(1)}, u32[]{:S(2)}, u32[]{:S(2)}) collective-permute-start(bf16[2048,128]{1,0:T(8,128)(2,1)S(1)} %collective-permute-done.2.refs_4_), channel_id=1, source_target_pairs={{0,4},{4,0},{8,12},{12,8},{16,20},{20,16},{24,28},{28,24},{32,36},... | collective-permute-start | bytes 1572872 | tf_op jit(solution)/shard_map/ppermute | solution.py:203

commit v5 on v4

--- a/solution.py
+++ b/solution.py
@@ -52,16 +52,20 @@
     )(grads)
 
 
-def fold(total):
-    wide = total.shape[0]
+def fold(totals):
+    wide = totals[0].shape[0]
     i = lax.broadcasted_iota(jnp.int32, (wide, wide), 0)
     j = lax.broadcasted_iota(jnp.int32, (wide, wide), 1)
-    kept = jnp.where(i % PACK == j % PACK, total, 0.0)
+    same = i % PACK == j % PACK
+    groups = wide // PACK
+    rows = [jnp.where(same, total, 0.0).reshape(groups, PACK, wide).sum(axis=1) for total in totals]
     k = lax.broadcasted_iota(jnp.int32, (wide, LANES), 0)
     s = lax.broadcasted_iota(jnp.int32, (wide, LANES), 1)
     pick = jnp.where(k // PACK == s, 1.0, 0.0)
-    columns = jnp.dot(kept, pick, precision=lax.Precision.HIGHEST, preferred_element_type=jnp.float32)
-    return columns.reshape(wide // PACK, PACK, LANES).sum(axis=1)
+    folded = jnp.dot(
+        jnp.concatenate(rows, axis=0), pick, precision=lax.Precision.HIGHEST, preferred_element_type=jnp.float32
+    )
+    return [folded[n * groups : (n + 1) * groups] for n in range(len(totals))]
 
 
 def grid_of(rows):
@@ -93,7 +97,7 @@
         low, high = group(0, part), group(half, part)
         found = (product(low, low), product(high, low), product(high, high))
         totals = found if totals is None else tuple(a + b for a, b in zip(totals, found))
-    low_low, high_low, high_high = (fold(t) for t in totals)
+    low_low, high_low, high_high = fold(totals)
     i, s = grid_of(half)
 
     def squares(gram):

time: 175 us -> 173 us (0.989)
  no operation moved by 1% of the time
where the time goes in v5:
time: 173 us
  blocking collectives  122 us (71%)
  starting transfers between devices  19 us (11%)
  Pallas kernels  18.3 us (11%)
  waiting for transfers between devices  12.3 us (7%)
    all_to_all x1, blocking collectives, body(): lax.all_to_all(slab, 'rep', split_axis=0, concat_axis=0, tiled=True)  105 us
    all_to_all x1, blocking collectives, body(): lax.all_to_all(jnp.broadcast_to(part[None], (everyone, SHORT, LANES)), ('...  17 us
    ppermute x9, waiting for transfers between devices, send(): return lax.ppermute(array, 'rep', pairs)  11.2 us
    ppermute x9, starting transfers between devices, send(): return lax.ppermute(array, 'rep', pairs)  10.4 us
    ppermute x8, starting transfers between devices, swap(): return lax.ppermute(array, 'rep', [(i, i ^ 1) for i in range(COUNT)])  8.59 us
    pallas_call x1, Pallas kernels, compact(): pl.pallas_call(functools.partial(compact_kernel, parts, 512), in_specs=[A...  6.09 us
    pallas_call x4, Pallas kernels, place(): pl.pallas_call(functools.partial(place_kernel, moves, rows), in_specs=[WH...  5.53 us
    pallas_call x1, Pallas kernels, partial_distances(): pl.pallas_call(functools.partial(distance_kernel, parts), in_specs=[WHOLE...  3.93 us
  transfers between devices with their start and end apart: 17, of which 6 were waited for; matrix products, arithmetic and copies ran while one was open for 0% of the time, Pallas kernels for 3%

profile of v5, /device:TPU:1, one launch (start us, length us, event | category | flops | bytes accessed | tf_op | source)
XLA Modules:
  0.0 173.0 jit_solution(5969683481459067715)
XLA Ops:
  0.6 6.1 %shard_map.30 = bf16[32768,128]{1,0:T(8,128)(2,1)S(1)} custom-call(bf16[1,4194304]{1,0:T(2,128)(2,1)} %x_ref.1), custom_call_target="tpu_custom_call" | custom-call | bytes 25165824 | tf_op jit(solution)/shard_map/pallas_call | solution.py:44
  6.7 105.0 %all_to_all.10.x_ref = bf16[32,1024,128]{2,1,0:T(8,128)(2,1)S(1)} all-to-all(bf16[32,1024,128]{2,1,0:T(8,128)(2,1)S(1)} %bitcast.4), channel_id=1, replica_groups=mesh['rep'=32,'shard'=4] {'rep'}, dimensions={0} | all-to-all | bytes 16777216 | tf_op jit(solution)/shard_map/all_to_all | solution.py:284
  111.7 3.9 %shard_map.31 = f32[4,128]{1,0:T(4,128)S(1)} custom-call(bf16[32,1024,128]{2,1,0:T(8,128)(2,1)S(1)} %all_to_all.10.x_ref), custom_call_target="tpu_custom_call" | custom-call | tf_op jit(solution)/shard_map/pallas_call | solution.py:122
  115.7 17.0 %all_to_all.11.d_ref = f32[128,4,128]{2,1,0:T(4,128)S(1)} all-to-all(f32[128,4,128]{2,1,0:T(4,128)S(1)} %broadcast_in_dim.2), channel_id=1, replica_groups=mesh['rep'=32,'shard'=4] {'rep','shard'}, dimensions={0} | all-to-all | bytes 524288 | tf_op jit(solution)/shard_map/all_to_all | solution.py:287
  132.6 2.8 %shard_map.32 = (bf16[1024,128]{1,0:T(8,128)(2,1)S(1)}, f32[1,128]{1,0:T(1,128)S(1)}) custom-call(f32[128,4,128]{2,1,0:T(4,128)S(1)} %all_to_all.11.d_ref, bf16[32,1024,128]{2,1,0:T(8,128)(2,1)S(1)} %all_to_all.10.x_ref), custom_call_target="tpu_custom_call" | custom-call | tf_op jit(solution)/shard_map/pallas_call | solution.py:182
  135.4 0.1 collective-permute-start
  135.5 2.7 %collective-permute-start.4 = (bf16[1024,128]{1,0:T(8,128)(2,1)S(1)}, bf16[1024,128]{1,0:T(8,128)(2,1)S(1)}, u32[]{:S(2)}, u32[]{:S(2)}) collective-permute-start(bf16[1024,128]{1,0:T(8,128)(2,1)S(1)} %get-tuple-element.8), channel_id=1, source_target_pairs={{0,96},{4,28},{8,104},{12,4},{16,112},{20,12},{24,120},{28,20},{32... | collective-permute-start | bytes 786440 | tf_op jit(solution)/shard_map/ppermute | solution.py:203
  138.2 4.0 %collective-permute-done = bf16[1024,128]{1,0:T(8,128)(2,1)S(1)} collective-permute-done((bf16[1024,128]{1,0:T(8,128)(2,1)S(1)}, bf16[1024,128]{1,0:T(8,128)(2,1)S(1)}, u32[]{:S(2)}, u32[]{:S(2)}) %collective-permute-start) | collective-permute-done | bytes 262176 | tf_op jit(solution)/shard_map/ppermute | solution.py:203
  142.3 1.2 collective-permute-start.8
  143.5 0.8 collective-permute-done.4
  144.3 0.9 collective-permute-done.5
  145.2 0.1 collective-permute-start.6
  145.4 2.6 %collective-permute-start.1 = (bf16[2048,128]{1,0:T(8,128)(2,1)S(1)}, bf16[2048,128]{1,0:T(8,128)(2,1)S(1)}, u32[]{:S(2)}, u32[]{:S(2)}) collective-permute-start(bf16[2048,128]{1,0:T(8,128)(2,1)S(1)} %constant_dynamic-update-slice_fusion.refs_0_), channel_id=1, source_target_pairs={{0,24},{4,100},{8,0},{12,108},{16,8},{20,116},{24,16},{28,124},{32... | collective-permute-start | bytes 1572872 | tf_op jit(solution)/shard_map/ppermute | solution.py:203
  148.0 2.2 %collective-permute-start.9 = (bf16[2048,128]{1,0:T(8,128)(2,1)S(1)}, bf16[2048,128]{1,0:T(8,128)(2,1)S(1)}, u32[]{:S(2)}, u32[]{:S(2)}) collective-permute-start(bf16[2048,128]{1,0:T(8,128)(2,1)S(1)} %constant_dynamic-update-slice_fusion.2.refs_1_), channel_id=1, source_target_pairs={{0,4},{4,0},{8,12},{12,8},{16,20},{20,16},{24,28},{28,24},{32,36},... | collective-permute-start | bytes 1572872 | tf_op jit(solution)/shard_map/ppermute | solution.py:207
  150.2 2.3 %collective-permute-start.7 = (bf16[2048,128]{1,0:T(8,128)(2,1)S(1)}, bf16[2048,128]{1,0:T(8,128)(2,1)S(1)}, u32[]{:S(2)}, u32[]{:S(2)}) collective-permute-start(bf16[2048,128]{1,0:T(8,128)(2,1)S(1)} %constant_dynamic-update-slice_fusion.2.refs_1_), channel_id=1, source_target_pairs={{0,24},{4,100},{8,0},{12,108},{16,8},{20,116},{24,16},{28,124},{32... | collective-permute-start | bytes 1572872 | tf_op jit(solution)/shard_map/ppermute | solution.py:203
  152.5 0.0 collective-permute-start.3
  152.5 2.3 %collective-permute-done.6.refs_2_ = bf16[2048,128]{1,0:T(8,128)(2,1)S(1)} collective-permute-done((bf16[2048,128]{1,0:T(8,128)(2,1)S(1)}, bf16[2048,128]{1,0:T(8,128)(2,1)S(1)}, u32[]{:S(2)}, u32[]{:S(2)}) %collective-permute-start.6) | collective-permute-done | bytes 524320 | tf_op jit(solution)/shard_map/ppermute | solution.py:203
  154.9 0.0 collective-permute-start.11
  154.9 0.5 slice_bitcast_fusion
  155.4 2.7 %collective-permute-start.2 = (bf16[2048,128]{1,0:T(8,128)(2,1)S(1)}, bf16[2048,128]{1,0:T(8,128)(2,1)S(1)}, u32[]{:S(2)}, u32[]{:S(2)}) collective-permute-start(bf16[2048,128]{1,0:T(8,128)(2,1)S(1)} %collective-permute-done.1.refs_1_), channel_id=1, source_target_pairs={{0,24},{4,100},{8,0},{12,108},{16,8},{20,116},{24,16},{28,124},{32... | collective-permute-start | bytes 1572872 | tf_op jit(solution)/shard_map/ppermute | solution.py:203
  158.0 1.4 shard_map.33.refs_4_
  159.4 3.2 %collective-permute-start.15 = (bf16[2048,128]{1,0:T(8,128)(2,1)S(1)}, bf16[2048,128]{1,0:T(8,128)(2,1)S(1)}, u32[]{:S(2)}, u32[]{:S(2)}) collective-permute-start(bf16[2048,128]{1,0:T(8,128)(2,1)S(1)} %collective-permute-done.6.refs_2_), channel_id=1, source_target_pairs={{0,4},{4,0},{8,12},{12,8},{16,20},{20,16},{24,28},{28,24},{32,36},... | collective-permute-start | bytes 1572872 | tf_op jit(solution)/shard_map/ppermute | solution.py:207
  162.6 0.1 collective-permute-start.16
  162.7 0.4 collective-permute-start.14
  163.1 1.4 shard_map.34.refs_6_
  164.5 3.2 %collective-permute-done.11.refs_5_ = bf16[2048,128]{1,0:T(8,128)(2,1)S(1)} collective-permute-done((bf16[2048,128]{1,0:T(8,128)(2,1)S(1)}, bf16[2048,128]{1,0:T(8,128)(2,1)S(1)}, u32[]{:S(2)}, u32[]{:S(2)}) %collective-permute-start.11) | collective-permute-done | bytes 524320 | tf_op jit(solution)/shard_map/ppermute | solution.py:203
  167.7 1.0 collective-permute-start.13
  168.6 0.0 collective-permute-start.12
  168.6 0.5 collective-permute-start.10
  169.1 1.0 collective-permute-done.13.refs_0_
  170.2 1.8 %shard_map.35.refs_2_ = bf16[32768,128]{1,0:T(8,128)(2,1)} custom-call(bf16[2048,128]{1,0:T(8,128)(2,1)S(1)} %collective-permute-done.13.refs_0_, bf16[2048,128]{1,0:T(8,128)(2,1)S(1)} %collective-permute-done.14.refs_1_, bf16[2048,128]{1,0:T(8,128)(2,1)S(1)} %collective-permute-done.15.refs_2_, ...), custom_call_target="tpu_custom_call", output_to_operand_aliasing={{}: (6, {})} | custom-call | bytes 3145728 | tf_op jit(solution)/shard_map/pallas_call | solution.py:232
  171.9 1.0 shard_map.36
  (17 shorter events, 0.2 us)
Async XLA Ops:
  135.4 6.8 %collective-permute-start = (bf16[1024,128]{1,0:T(8,128)(2,1)S(1)}, bf16[1024,128]{1,0:T(8,128)(2,1)S(1)}, u32[]{:S(2)}, u32[]{:S(2)}) collective-permute-start(bf16[1024,128]{1,0:T(8,128)(2,1)S(1)} %get-tuple-element.8), channel_id=1, source_target_pairs={{0,32},{4,12},{8,40},{12,20},{16,48},{20,28},{24,56},{28,4},{32,64... | collective-permute-start | bytes 786440 | tf_op jit(solution)/shard_map/ppermute | solution.py:203
  135.5 8.8 %collective-permute-start.4 = (bf16[1024,128]{1,0:T(8,128)(2,1)S(1)}, bf16[1024,128]{1,0:T(8,128)(2,1)S(1)}, u32[]{:S(2)}, u32[]{:S(2)}) collective-permute-start(bf16[1024,128]{1,0:T(8,128)(2,1)S(1)} %get-tuple-element.8), channel_id=1, source_target_pairs={{0,96},{4,28},{8,104},{12,4},{16,112},{20,12},{24,120},{28,20},{32... | collective-permute-start | bytes 786440 | tf_op jit(solution)/shard_map/ppermute | solution.py:203
  138.2 7.0 %collective-permute-start.5 = (bf16[1024,128]{1,0:T(8,128)(2,1)S(1)}, bf16[1024,128]{1,0:T(8,128)(2,1)S(1)}, u32[]{:S(2)}, u32[]{:S(2)}) collective-permute-start(bf16[1024,128]{1,0:T(8,128)(2,1)S(1)} %get-tuple-element.8), channel_id=1, source_target_pairs={{0,64},{4,20},{8,72},{12,28},{16,80},{20,4},{24,88},{28,12},{32,96... | collective-permute-start | bytes 786440 | tf_op jit(solution)/shard_map/ppermute | solution.py:203
  142.3 10.2 %collective-permute-start.8 = (bf16[2048,128]{1,0:T(8,128)(2,1)S(1)}, bf16[2048,128]{1,0:T(8,128)(2,1)S(1)}, u32[]{:S(2)}, u32[]{:S(2)}) collective-permute-start(bf16[2048,128]{1,0:T(8,128)(2,1)S(1)} %constant_dynamic-update-slice_fusion.refs_0_), channel_id=1, source_target_pairs={{0,4},{4,0},{8,12},{12,8},{16,20},{20,16},{24,28},{28,24},{32,36},... | collective-permute-start | bytes 1572872 | tf_op jit(solution)/shard_map/ppermute | solution.py:207
  145.2 9.6 %collective-permute-start.6 = (bf16[2048,128]{1,0:T(8,128)(2,1)S(1)}, bf16[2048,128]{1,0:T(8,128)(2,1)S(1)}, u32[]{:S(2)}, u32[]{:S(2)}) collective-permute-start(bf16[2048,128]{1,0:T(8,128)(2,1)S(1)} %constant_dynamic-update-slice_fusion.2.refs_1_), channel_id=1, source_target_pairs={{0,8},{4,36},{8,16},{12,44},{16,24},{20,52},{24,0},{28,60},{32,40}... | collective-permute-start | bytes 1572872 | tf_op jit(solution)/shard_map/ppermute | solution.py:203
  145.4 10.0 %collective-permute-start.1 = (bf16[2048,128]{1,0:T(8,128)(2,1)S(1)}, bf16[2048,128]{1,0:T(8,128)(2,1)S(1)}, u32[]{:S(2)}, u32[]{:S(2)}) collective-permute-start(bf16[2048,128]{1,0:T(8,128)(2,1)S(1)} %constant_dynamic-update-slice_fusion.refs_0_), channel_id=1, source_target_pairs={{0,24},{4,100},{8,0},{12,108},{16,8},{20,116},{24,16},{28,124},{32... | collective-permute-start | bytes 1572872 | tf_op jit(solution)/shard_map/ppermute | solution.py:203
  148.0 10.1 %collective-permute-start.9 = (bf16[2048,128]{1,0:T(8,128)(2,1)S(1)}, bf16[2048,128]{1,0:T(8,128)(2,1)S(1)}, u32[]{:S(2)}, u32[]{:S(2)}) collective-permute-start(bf16[2048,128]{1,0:T(8,128)(2,1)S(1)} %constant_dynamic-update-slice_fusion.2.refs_1_), channel_id=1, source_target_pairs={{0,4},{4,0},{8,12},{12,8},{16,20},{20,16},{24,28},{28,24},{32,36},... | collective-permute-start | bytes 1572872 | tf_op jit(solution)/shard_map/ppermute | solution.py:207
  150.2 12.4 %collective-permute-start.7 = (bf16[2048,128]{1,0:T(8,128)(2,1)S(1)}, bf16[2048,128]{1,0:T(8,128)(2,1)S(1)}, u32[]{:S(2)}, u32[]{:S(2)}) collective-permute-start(bf16[2048,128]{1,0:T(8,128)(2,1)S(1)} %constant_dynamic-update-slice_fusion.2.refs_1_), channel_id=1, source_target_pairs={{0,24},{4,100},{8,0},{12,108},{16,8},{20,116},{24,16},{28,124},{32... | collective-permute-start | bytes 1572872 | tf_op jit(solution)/shard_map/ppermute | solution.py:203
  152.5 10.2 %collective-permute-start.3 = (bf16[2048,128]{1,0:T(8,128)(2,1)S(1)}, bf16[2048,128]{1,0:T(8,128)(2,1)S(1)}, u32[]{:S(2)}, u32[]{:S(2)}) collective-permute-start(bf16[2048,128]{1,0:T(8,128)(2,1)S(1)} %constant_dynamic-update-slice_fusion.refs_0_), channel_id=1, source_target_pairs={{0,8},{4,36},{8,16},{12,44},{16,24},{20,52},{24,0},{28,60},{32,40}... | collective-permute-start | bytes 1572872 | tf_op jit(solution)/shard_map/ppermute | solution.py:203
  154.9 12.8 %collective-permute-start.11 = (bf16[2048,128]{1,0:T(8,128)(2,1)S(1)}, bf16[2048,128]{1,0:T(8,128)(2,1)S(1)}, u32[]{:S(2)}, u32[]{:S(2)}) collective-permute-start(bf16[2048,128]{1,0:T(8,128)(2,1)S(1)} %collective-permute-done.6.refs_2_), channel_id=1, source_target_pairs={{0,8},{4,36},{8,16},{12,44},{16,24},{20,52},{24,0},{28,60},{32,40}... | collective-permute-start | bytes 1572872 | tf_op jit(solution)/shard_map/ppermute | solution.py:203
  155.4 13.3 %collective-permute-start.2 = (bf16[2048,128]{1,0:T(8,128)(2,1)S(1)}, bf16[2048,128]{1,0:T(8,128)(2,1)S(1)}, u32[]{:S(2)}, u32[]{:S(2)}) collective-permute-start(bf16[2048,128]{1,0:T(8,128)(2,1)S(1)} %collective-permute-done.1.refs_1_), channel_id=1, source_target_pairs={{0,24},{4,100},{8,0},{12,108},{16,8},{20,116},{24,16},{28,124},{32... | collective-permute-start | bytes 1572872 | tf_op jit(solution)/shard_map/ppermute | solution.py:203
  159.4 9.2 %collective-permute-start.15 = (bf16[2048,128]{1,0:T(8,128)(2,1)S(1)}, bf16[2048,128]{1,0:T(8,128)(2,1)S(1)}, u32[]{:S(2)}, u32[]{:S(2)}) collective-permute-start(bf16[2048,128]{1,0:T(8,128)(2,1)S(1)} %collective-permute-done.6.refs_2_), channel_id=1, source_target_pairs={{0,4},{4,0},{8,12},{12,8},{16,20},{20,16},{24,28},{28,24},{32,36},... | collective-permute-start | bytes 1572872 | tf_op jit(solution)/shard_map/ppermute | solution.py:207
  162.6 6.5 %collective-permute-start.16 = (bf16[2048,128]{1,0:T(8,128)(2,1)S(1)}, bf16[2048,128]{1,0:T(8,128)(2,1)S(1)}, u32[]{:S(2)}, u32[]{:S(2)}) collective-permute-start(bf16[2048,128]{1,0:T(8,128)(2,1)S(1)} %collective-permute-done.7.refs_3_), channel_id=1, source_target_pairs={{0,4},{4,0},{8,12},{12,8},{16,20},{20,16},{24,28},{28,24},{32,36},... | collective-permute-start | bytes 1572872 | tf_op jit(solution)/shard_map/ppermute | solution.py:207
  162.7 6.4 %collective-permute-start.14 = (bf16[2048,128]{1,0:T(8,128)(2,1)S(1)}, bf16[2048,128]{1,0:T(8,128)(2,1)S(1)}, u32[]{:S(2)}, u32[]{:S(2)}) collective-permute-start(bf16[2048,128]{1,0:T(8,128)(2,1)S(1)} %collective-permute-done.1.refs_1_), channel_id=1, source_target_pairs={{0,4},{4,0},{8,12},{12,8},{16,20},{20,16},{24,28},{28,24},{32,36},... | collective-permute-start | bytes 1572872 | tf_op jit(solution)/shard_map/ppermute | solution.py:207
  167.7 2.5 %collective-permute-start.13 = (bf16[2048,128]{1,0:T(8,128)(2,1)S(1)}, bf16[2048,128]{1,0:T(8,128)(2,1)S(1)}, u32[]{:S(2)}, u32[]{:S(2)}) collective-permute-start(bf16[2048,128]{1,0:T(8,128)(2,1)S(1)} %collective-permute-done.3.refs_0_), channel_id=1, source_target_pairs={{0,4},{4,0},{8,12},{12,8},{16,20},{20,16},{24,28},{28,24},{32,36},... | collective-permute-start | bytes 1572872 | tf_op jit(solution)/shard_map/ppermute | solution.py:207
  168.6 3.3 %collective-permute-start.12 = (bf16[2048,128]{1,0:T(8,128)(2,1)S(1)}, bf16[2048,128]{1,0:T(8,128)(2,1)S(1)}, u32[]{:S(2)}, u32[]{:S(2)}) collective-permute-start(bf16[2048,128]{1,0:T(8,128)(2,1)S(1)} %collective-permute-done.11.refs_5_), channel_id=1, source_target_pairs={{0,4},{4,0},{8,12},{12,8},{16,20},{20,16},{24,28},{28,24},{32,36},... | collective-permute-start | bytes 1572872 | tf_op jit(solution)/shard_map/ppermute | solution.py:207
  168.6 3.3 %collective-permute-start.10 = (bf16[2048,128]{1,0:T(8,128)(2,1)S(1)}, bf16[2048,128]{1,0:T(8,128)(2,1)S(1)}, u32[]{:S(2)}, u32[]{:S(2)}) collective-permute-start(bf16[2048,128]{1,0:T(8,128)(2,1)S(1)} %collective-permute-done.2.refs_4_), channel_id=1, source_target_pairs={{0,4},{4,0},{8,12},{12,8},{16,20},{20,16},{24,28},{28,24},{32,36},... | collective-permute-start | bytes 1572872 | tf_op jit(solution)/shard_map/ppermute | solution.py:207

commit v6 on v5

--- a/solution.py
+++ b/solution.py
@@ -160,12 +160,22 @@
     return weights, jnp.sum(same * weights, axis=0, keepdims=True)
 
 
+def add_up(ref, ways=8):
+    each = ref.shape[0] // ways
+    sums = [ref[n * each] for n in range(ways)]
+    for k in range(1, each):
+        sums = [total + ref[n * each + k] for n, total in enumerate(sums)]
+    while len(sums) > 1:
+        sums = [a + b for a, b in zip(sums[::2], sums[1::2])]
+    return sums[0]
+
+
 def aggregate_kernel(total, d_ref, x_ref, o_ref, w_ref, coeffs):
     count, rows, _ = x_ref.shape
-    weights, across = weiszfeld(all_distances(d_ref[...].sum(axis=0), count), total)
+    weights, across = weiszfeld(all_distances(add_up(d_ref), count), total)
     w_ref[...] = across
     coeffs[...] = jnp.broadcast_to(weights.astype(jnp.bfloat16).astype(jnp.float32), (count, LANES))
-    piece = 32
+    piece = 64
 
     @pl.loop(0, rows // piece)
     def _(k):

time: 173 us -> 173 us (level)
  no operation moved by 1% of the time
where the time goes in v6:
time: 173 us
  blocking collectives  122 us (71%)
  starting transfers between devices  19 us (11%)
  Pallas kernels  18.1 us (10%)
  waiting for transfers between devices  12.3 us (7%)
    all_to_all x1, blocking collectives, body(): lax.all_to_all(slab, 'rep', split_axis=0, concat_axis=0, tiled=True)  105 us
    all_to_all x1, blocking collectives, body(): lax.all_to_all(jnp.broadcast_to(part[None], (everyone, SHORT, LANES)), ('...  17 us
    ppermute x9, waiting for transfers between devices, send(): return lax.ppermute(array, 'rep', pairs)  11.2 us
    ppermute x9, starting transfers between devices, send(): return lax.ppermute(array, 'rep', pairs)  10.4 us
    ppermute x8, starting transfers between devices, swap(): return lax.ppermute(array, 'rep', [(i, i ^ 1) for i in range(COUNT)])  8.59 us
    pallas_call x1, Pallas kernels, compact(): pl.pallas_call(functools.partial(compact_kernel, parts, 512), in_specs=[A...  6.09 us
    pallas_call x4, Pallas kernels, place(): pl.pallas_call(functools.partial(place_kernel, moves, rows), in_specs=[WH...  5.53 us
    pallas_call x1, Pallas kernels, partial_distances(): pl.pallas_call(functools.partial(distance_kernel, parts), in_specs=[WHOLE...  3.93 us
  transfers between devices with their start and end apart: 17, of which 6 were waited for; matrix products, arithmetic and copies ran while one was open for 0% of the time, Pallas kernels for 3%

profile of v6, /device:TPU:1, one launch (start us, length us, event | category | flops | bytes accessed | tf_op | source)
XLA Modules:
  0.0 172.8 jit_solution(3648420675041212544)
XLA Ops:
  0.6 6.1 %shard_map.30 = bf16[32768,128]{1,0:T(8,128)(2,1)S(1)} custom-call(bf16[1,4194304]{1,0:T(2,128)(2,1)} %x_ref.1), custom_call_target="tpu_custom_call" | custom-call | bytes 25165824 | tf_op jit(solution)/shard_map/pallas_call | solution.py:44
  6.7 105.0 %all_to_all.10.x_ref = bf16[32,1024,128]{2,1,0:T(8,128)(2,1)S(1)} all-to-all(bf16[32,1024,128]{2,1,0:T(8,128)(2,1)S(1)} %bitcast.4), channel_id=1, replica_groups=mesh['rep'=32,'shard'=4] {'rep'}, dimensions={0} | all-to-all | bytes 16777216 | tf_op jit(solution)/shard_map/all_to_all | solution.py:294
  111.7 3.9 %shard_map.31 = f32[4,128]{1,0:T(4,128)S(1)} custom-call(bf16[32,1024,128]{2,1,0:T(8,128)(2,1)S(1)} %all_to_all.10.x_ref), custom_call_target="tpu_custom_call" | custom-call | tf_op jit(solution)/shard_map/pallas_call | solution.py:122
  115.7 17.0 %all_to_all.11.d_ref = f32[128,4,128]{2,1,0:T(4,128)S(1)} all-to-all(f32[128,4,128]{2,1,0:T(4,128)S(1)} %broadcast_in_dim.2), channel_id=1, replica_groups=mesh['rep'=32,'shard'=4] {'rep','shard'}, dimensions={0} | all-to-all | bytes 524288 | tf_op jit(solution)/shard_map/all_to_all | solution.py:297
  132.6 2.6 %shard_map.32 = (bf16[1024,128]{1,0:T(8,128)(2,1)S(1)}, f32[1,128]{1,0:T(1,128)S(1)}) custom-call(f32[128,4,128]{2,1,0:T(4,128)S(1)} %all_to_all.11.d_ref, bf16[32,1024,128]{2,1,0:T(8,128)(2,1)S(1)} %all_to_all.10.x_ref), custom_call_target="tpu_custom_call" | custom-call | tf_op jit(solution)/shard_map/pallas_call | solution.py:192
  135.2 0.1 collective-permute-start
  135.3 2.7 %collective-permute-start.4 = (bf16[1024,128]{1,0:T(8,128)(2,1)S(1)}, bf16[1024,128]{1,0:T(8,128)(2,1)S(1)}, u32[]{:S(2)}, u32[]{:S(2)}) collective-permute-start(bf16[1024,128]{1,0:T(8,128)(2,1)S(1)} %get-tuple-element.8), channel_id=1, source_target_pairs={{0,96},{4,28},{8,104},{12,4},{16,112},{20,12},{24,120},{28,20},{32... | collective-permute-start | bytes 786440 | tf_op jit(solution)/shard_map/ppermute | solution.py:213
  138.0 0.0 collective-permute-start.5
  138.0 4.0 %collective-permute-done = bf16[1024,128]{1,0:T(8,128)(2,1)S(1)} collective-permute-done((bf16[1024,128]{1,0:T(8,128)(2,1)S(1)}, bf16[1024,128]{1,0:T(8,128)(2,1)S(1)}, u32[]{:S(2)}, u32[]{:S(2)}) %collective-permute-start) | collective-permute-done | bytes 262176 | tf_op jit(solution)/shard_map/ppermute | solution.py:213
  142.1 1.2 collective-permute-start.8
  143.3 0.8 collective-permute-done.4
  144.1 0.9 collective-permute-done.5
  145.0 0.1 collective-permute-start.6
  145.2 2.6 %collective-permute-start.1 = (bf16[2048,128]{1,0:T(8,128)(2,1)S(1)}, bf16[2048,128]{1,0:T(8,128)(2,1)S(1)}, u32[]{:S(2)}, u32[]{:S(2)}) collective-permute-start(bf16[2048,128]{1,0:T(8,128)(2,1)S(1)} %constant_dynamic-update-slice_fusion.refs_0_), channel_id=1, source_target_pairs={{0,24},{4,100},{8,0},{12,108},{16,8},{20,116},{24,16},{28,124},{32... | collective-permute-start | bytes 1572872 | tf_op jit(solution)/shard_map/ppermute | solution.py:213
  147.8 2.2 %collective-permute-start.9 = (bf16[2048,128]{1,0:T(8,128)(2,1)S(1)}, bf16[2048,128]{1,0:T(8,128)(2,1)S(1)}, u32[]{:S(2)}, u32[]{:S(2)}) collective-permute-start(bf16[2048,128]{1,0:T(8,128)(2,1)S(1)} %constant_dynamic-update-slice_fusion.2.refs_1_), channel_id=1, source_target_pairs={{0,4},{4,0},{8,12},{12,8},{16,20},{20,16},{24,28},{28,24},{32,36},... | collective-permute-start | bytes 1572872 | tf_op jit(solution)/shard_map/ppermute | solution.py:217
  150.0 2.3 %collective-permute-start.7 = (bf16[2048,128]{1,0:T(8,128)(2,1)S(1)}, bf16[2048,128]{1,0:T(8,128)(2,1)S(1)}, u32[]{:S(2)}, u32[]{:S(2)}) collective-permute-start(bf16[2048,128]{1,0:T(8,128)(2,1)S(1)} %constant_dynamic-update-slice_fusion.2.refs_1_), channel_id=1, source_target_pairs={{0,24},{4,100},{8,0},{12,108},{16,8},{20,116},{24,16},{28,124},{32... | collective-permute-start | bytes 1572872 | tf_op jit(solution)/shard_map/ppermute | solution.py:213
  152.3 0.0 collective-permute-done.8.refs_2_
  152.3 2.3 %collective-permute-done.6.refs_2_ = bf16[2048,128]{1,0:T(8,128)(2,1)S(1)} collective-permute-done((bf16[2048,128]{1,0:T(8,128)(2,1)S(1)}, bf16[2048,128]{1,0:T(8,128)(2,1)S(1)}, u32[]{:S(2)}, u32[]{:S(2)}) %collective-permute-start.6) | collective-permute-done | bytes 524320 | tf_op jit(solution)/shard_map/ppermute | solution.py:213
  154.7 0.5 slice_bitcast_fusion
  155.2 2.7 %collective-permute-start.2 = (bf16[2048,128]{1,0:T(8,128)(2,1)S(1)}, bf16[2048,128]{1,0:T(8,128)(2,1)S(1)}, u32[]{:S(2)}, u32[]{:S(2)}) collective-permute-start(bf16[2048,128]{1,0:T(8,128)(2,1)S(1)} %collective-permute-done.1.refs_1_), channel_id=1, source_target_pairs={{0,24},{4,100},{8,0},{12,108},{16,8},{20,116},{24,16},{28,124},{32... | collective-permute-start | bytes 1572872 | tf_op jit(solution)/shard_map/ppermute | solution.py:213
  157.8 1.4 shard_map.33.refs_4_
  159.2 3.2 %collective-permute-start.15 = (bf16[2048,128]{1,0:T(8,128)(2,1)S(1)}, bf16[2048,128]{1,0:T(8,128)(2,1)S(1)}, u32[]{:S(2)}, u32[]{:S(2)}) collective-permute-start(bf16[2048,128]{1,0:T(8,128)(2,1)S(1)} %collective-permute-done.6.refs_2_), channel_id=1, source_target_pairs={{0,4},{4,0},{8,12},{12,8},{16,20},{20,16},{24,28},{28,24},{32,36},... | collective-permute-start | bytes 1572872 | tf_op jit(solution)/shard_map/ppermute | solution.py:217
  162.4 0.1 collective-permute-start.16
  162.5 0.4 collective-permute-start.14
  162.9 1.4 shard_map.34.refs_6_
  164.3 3.2 %collective-permute-done.11.refs_5_ = bf16[2048,128]{1,0:T(8,128)(2,1)S(1)} collective-permute-done((bf16[2048,128]{1,0:T(8,128)(2,1)S(1)}, bf16[2048,128]{1,0:T(8,128)(2,1)S(1)}, u32[]{:S(2)}, u32[]{:S(2)}) %collective-permute-start.11) | collective-permute-done | bytes 524320 | tf_op jit(solution)/shard_map/ppermute | solution.py:213
  167.5 1.0 collective-permute-start.13
  168.4 0.0 collective-permute-start.12
  168.4 0.5 collective-permute-start.10
  168.9 1.0 collective-permute-done.13.refs_0_
  170.0 1.8 %shard_map.35.refs_2_ = bf16[32768,128]{1,0:T(8,128)(2,1)} custom-call(bf16[2048,128]{1,0:T(8,128)(2,1)S(1)} %collective-permute-done.13.refs_0_, bf16[2048,128]{1,0:T(8,128)(2,1)S(1)} %collective-permute-done.14.refs_1_, bf16[2048,128]{1,0:T(8,128)(2,1)S(1)} %collective-permute-done.15.refs_2_, ...), custom_call_target="tpu_custom_call", output_to_operand_aliasing={{}: (6, {})} | custom-call | bytes 3145728 | tf_op jit(solution)/shard_map/pallas_call | solution.py:242
  171.7 1.0 shard_map.36
  (17 shorter events, 0.2 us)
Async XLA Ops:
  135.2 6.8 %collective-permute-start = (bf16[1024,128]{1,0:T(8,128)(2,1)S(1)}, bf16[1024,128]{1,0:T(8,128)(2,1)S(1)}, u32[]{:S(2)}, u32[]{:S(2)}) collective-permute-start(bf16[1024,128]{1,0:T(8,128)(2,1)S(1)} %get-tuple-element.8), channel_id=1, source_target_pairs={{0,32},{4,12},{8,40},{12,20},{16,48},{20,28},{24,56},{28,4},{32,64... | collective-permute-start | bytes 786440 | tf_op jit(solution)/shard_map/ppermute | solution.py:213
  135.3 8.8 %collective-permute-start.4 = (bf16[1024,128]{1,0:T(8,128)(2,1)S(1)}, bf16[1024,128]{1,0:T(8,128)(2,1)S(1)}, u32[]{:S(2)}, u32[]{:S(2)}) collective-permute-start(bf16[1024,128]{1,0:T(8,128)(2,1)S(1)} %get-tuple-element.8), channel_id=1, source_target_pairs={{0,96},{4,28},{8,104},{12,4},{16,112},{20,12},{24,120},{28,20},{32... | collective-permute-start | bytes 786440 | tf_op jit(solution)/shard_map/ppermute | solution.py:213
  138.0 7.0 %collective-permute-start.5 = (bf16[1024,128]{1,0:T(8,128)(2,1)S(1)}, bf16[1024,128]{1,0:T(8,128)(2,1)S(1)}, u32[]{:S(2)}, u32[]{:S(2)}) collective-permute-start(bf16[1024,128]{1,0:T(8,128)(2,1)S(1)} %get-tuple-element.8), channel_id=1, source_target_pairs={{0,64},{4,20},{8,72},{12,28},{16,80},{20,4},{24,88},{28,12},{32,96... | collective-permute-start | bytes 786440 | tf_op jit(solution)/shard_map/ppermute | solution.py:213
  142.1 10.2 %collective-permute-start.8 = (bf16[2048,128]{1,0:T(8,128)(2,1)S(1)}, bf16[2048,128]{1,0:T(8,128)(2,1)S(1)}, u32[]{:S(2)}, u32[]{:S(2)}) collective-permute-start(bf16[2048,128]{1,0:T(8,128)(2,1)S(1)} %constant_dynamic-update-slice_fusion.refs_0_), channel_id=1, source_target_pairs={{0,4},{4,0},{8,12},{12,8},{16,20},{20,16},{24,28},{28,24},{32,36},... | collective-permute-start | bytes 1572872 | tf_op jit(solution)/shard_map/ppermute | solution.py:217
  145.0 9.6 %collective-permute-start.6 = (bf16[2048,128]{1,0:T(8,128)(2,1)S(1)}, bf16[2048,128]{1,0:T(8,128)(2,1)S(1)}, u32[]{:S(2)}, u32[]{:S(2)}) collective-permute-start(bf16[2048,128]{1,0:T(8,128)(2,1)S(1)} %constant_dynamic-update-slice_fusion.2.refs_1_), channel_id=1, source_target_pairs={{0,8},{4,36},{8,16},{12,44},{16,24},{20,52},{24,0},{28,60},{32,40}... | collective-permute-start | bytes 1572872 | tf_op jit(solution)/shard_map/ppermute | solution.py:213
  145.2 10.0 %collective-permute-start.1 = (bf16[2048,128]{1,0:T(8,128)(2,1)S(1)}, bf16[2048,128]{1,0:T(8,128)(2,1)S(1)}, u32[]{:S(2)}, u32[]{:S(2)}) collective-permute-start(bf16[2048,128]{1,0:T(8,128)(2,1)S(1)} %constant_dynamic-update-slice_fusion.refs_0_), channel_id=1, source_target_pairs={{0,24},{4,100},{8,0},{12,108},{16,8},{20,116},{24,16},{28,124},{32... | collective-permute-start | bytes 1572872 | tf_op jit(solution)/shard_map/ppermute | solution.py:213
  147.8 10.1 %collective-permute-start.9 = (bf16[2048,128]{1,0:T(8,128)(2,1)S(1)}, bf16[2048,128]{1,0:T(8,128)(2,1)S(1)}, u32[]{:S(2)}, u32[]{:S(2)}) collective-permute-start(bf16[2048,128]{1,0:T(8,128)(2,1)S(1)} %constant_dynamic-update-slice_fusion.2.refs_1_), channel_id=1, source_target_pairs={{0,4},{4,0},{8,12},{12,8},{16,20},{20,16},{24,28},{28,24},{32,36},... | collective-permute-start | bytes 1572872 | tf_op jit(solution)/shard_map/ppermute | solution.py:217
  150.0 12.4 %collective-permute-start.7 = (bf16[2048,128]{1,0:T(8,128)(2,1)S(1)}, bf16[2048,128]{1,0:T(8,128)(2,1)S(1)}, u32[]{:S(2)}, u32[]{:S(2)}) collective-permute-start(bf16[2048,128]{1,0:T(8,128)(2,1)S(1)} %constant_dynamic-update-slice_fusion.2.refs_1_), channel_id=1, source_target_pairs={{0,24},{4,100},{8,0},{12,108},{16,8},{20,116},{24,16},{28,124},{32... | collective-permute-start | bytes 1572872 | tf_op jit(solution)/shard_map/ppermute | solution.py:213
  152.3 10.2 %collective-permute-start.3 = (bf16[2048,128]{1,0:T(8,128)(2,1)S(1)}, bf16[2048,128]{1,0:T(8,128)(2,1)S(1)}, u32[]{:S(2)}, u32[]{:S(2)}) collective-permute-start(bf16[2048,128]{1,0:T(8,128)(2,1)S(1)} %constant_dynamic-update-slice_fusion.refs_0_), channel_id=1, source_target_pairs={{0,8},{4,36},{8,16},{12,44},{16,24},{20,52},{24,0},{28,60},{32,40}... | collective-permute-start | bytes 1572872 | tf_op jit(solution)/shard_map/ppermute | solution.py:213
  154.6 12.8 %collective-permute-start.11 = (bf16[2048,128]{1,0:T(8,128)(2,1)S(1)}, bf16[2048,128]{1,0:T(8,128)(2,1)S(1)}, u32[]{:S(2)}, u32[]{:S(2)}) collective-permute-start(bf16[2048,128]{1,0:T(8,128)(2,1)S(1)} %collective-permute-done.6.refs_2_), channel_id=1, source_target_pairs={{0,8},{4,36},{8,16},{12,44},{16,24},{20,52},{24,0},{28,60},{32,40}... | collective-permute-start | bytes 1572872 | tf_op jit(solution)/shard_map/ppermute | solution.py:213
  155.2 13.3 %collective-permute-start.2 = (bf16[2048,128]{1,0:T(8,128)(2,1)S(1)}, bf16[2048,128]{1,0:T(8,128)(2,1)S(1)}, u32[]{:S(2)}, u32[]{:S(2)}) collective-permute-start(bf16[2048,128]{1,0:T(8,128)(2,1)S(1)} %collective-permute-done.1.refs_1_), channel_id=1, source_target_pairs={{0,24},{4,100},{8,0},{12,108},{16,8},{20,116},{24,16},{28,124},{32... | collective-permute-start | bytes 1572872 | tf_op jit(solution)/shard_map/ppermute | solution.py:213
  159.2 9.2 %collective-permute-start.15 = (bf16[2048,128]{1,0:T(8,128)(2,1)S(1)}, bf16[2048,128]{1,0:T(8,128)(2,1)S(1)}, u32[]{:S(2)}, u32[]{:S(2)}) collective-permute-start(bf16[2048,128]{1,0:T(8,128)(2,1)S(1)} %collective-permute-done.6.refs_2_), channel_id=1, source_target_pairs={{0,4},{4,0},{8,12},{12,8},{16,20},{20,16},{24,28},{28,24},{32,36},... | collective-permute-start | bytes 1572872 | tf_op jit(solution)/shard_map/ppermute | solution.py:217
  162.4 6.5 %collective-permute-start.16 = (bf16[2048,128]{1,0:T(8,128)(2,1)S(1)}, bf16[2048,128]{1,0:T(8,128)(2,1)S(1)}, u32[]{:S(2)}, u32[]{:S(2)}) collective-permute-start(bf16[2048,128]{1,0:T(8,128)(2,1)S(1)} %collective-permute-done.7.refs_3_), channel_id=1, source_target_pairs={{0,4},{4,0},{8,12},{12,8},{16,20},{20,16},{24,28},{28,24},{32,36},... | collective-permute-start | bytes 1572872 | tf_op jit(solution)/shard_map/ppermute | solution.py:217
  162.5 6.4 %collective-permute-start.14 = (bf16[2048,128]{1,0:T(8,128)(2,1)S(1)}, bf16[2048,128]{1,0:T(8,128)(2,1)S(1)}, u32[]{:S(2)}, u32[]{:S(2)}) collective-permute-start(bf16[2048,128]{1,0:T(8,128)(2,1)S(1)} %collective-permute-done.1.refs_1_), channel_id=1, source_target_pairs={{0,4},{4,0},{8,12},{12,8},{16,20},{20,16},{24,28},{28,24},{32,36},... | collective-permute-start | bytes 1572872 | tf_op jit(solution)/shard_map/ppermute | solution.py:217
  167.5 2.5 %collective-permute-start.13 = (bf16[2048,128]{1,0:T(8,128)(2,1)S(1)}, bf16[2048,128]{1,0:T(8,128)(2,1)S(1)}, u32[]{:S(2)}, u32[]{:S(2)}) collective-permute-start(bf16[2048,128]{1,0:T(8,128)(2,1)S(1)} %collective-permute-done.3.refs_0_), channel_id=1, source_target_pairs={{0,4},{4,0},{8,12},{12,8},{16,20},{20,16},{24,28},{28,24},{32,36},... | collective-permute-start | bytes 1572872 | tf_op jit(solution)/shard_map/ppermute | solution.py:217
  168.4 3.3 %collective-permute-start.12 = (bf16[2048,128]{1,0:T(8,128)(2,1)S(1)}, bf16[2048,128]{1,0:T(8,128)(2,1)S(1)}, u32[]{:S(2)}, u32[]{:S(2)}) collective-permute-start(bf16[2048,128]{1,0:T(8,128)(2,1)S(1)} %collective-permute-done.11.refs_5_), channel_id=1, source_target_pairs={{0,4},{4,0},{8,12},{12,8},{16,20},{20,16},{24,28},{28,24},{32,36},... | collective-permute-start | bytes 1572872 | tf_op jit(solution)/shard_map/ppermute | solution.py:217
  168.4 3.3 %collective-permute-start.10 = (bf16[2048,128]{1,0:T(8,128)(2,1)S(1)}, bf16[2048,128]{1,0:T(8,128)(2,1)S(1)}, u32[]{:S(2)}, u32[]{:S(2)}) collective-permute-start(bf16[2048,128]{1,0:T(8,128)(2,1)S(1)} %collective-permute-done.2.refs_4_), channel_id=1, source_target_pairs={{0,4},{4,0},{8,12},{12,8},{16,20},{20,16},{24,28},{28,24},{32,36},... | collective-permute-start | bytes 1572872 | tf_op jit(solution)/shard_map/ppermute | solution.py:217

commit v7 on v6

--- a/solution.py
+++ b/solution.py
@@ -290,7 +290,7 @@
 def body(grads):
     count = lax.axis_size("rep")
     total = grads.shape[1] * lax.axis_size("shard")
-    slab = compact(grads, 8).reshape(count, -1, LANES)
+    slab = compact(grads, 16).reshape(count, -1, LANES)
     blocks = lax.all_to_all(slab, "rep", split_axis=0, concat_axis=0, tiled=True)
     part = partial_distances(blocks, 1)
     everyone = count * lax.axis_size("shard")

time: 173 us -> 173 us (level)
  no operation moved by 1% of the time
where the time goes in v7:
time: 173 us
  blocking collectives  122 us (71%)
  starting transfers between devices  19 us (11%)
  Pallas kernels  18 us (10%)
  waiting for transfers between devices  12.3 us (7%)
    all_to_all x1, blocking collectives, body(): lax.all_to_all(slab, 'rep', split_axis=0, concat_axis=0, tiled=True)  105 us
    all_to_all x1, blocking collectives, body(): lax.all_to_all(jnp.broadcast_to(part[None], (everyone, SHORT, LANES)), ('...  17 us
    ppermute x9, waiting for transfers between devices, send(): return lax.ppermute(array, 'rep', pairs)  11.2 us
    ppermute x9, starting transfers between devices, send(): return lax.ppermute(array, 'rep', pairs)  10.4 us
    ppermute x8, starting transfers between devices, swap(): return lax.ppermute(array, 'rep', [(i, i ^ 1) for i in range(COUNT)])  8.59 us
    pallas_call x1, Pallas kernels, compact(): pl.pallas_call(functools.partial(compact_kernel, parts, 512), in_specs=[A...  6.01 us
    pallas_call x4, Pallas kernels, place(): pl.pallas_call(functools.partial(place_kernel, moves, rows), in_specs=[WH...  5.53 us
    pallas_call x1, Pallas kernels, partial_distances(): pl.pallas_call(functools.partial(distance_kernel, parts), in_specs=[WHOLE...  3.92 us
  transfers between devices with their start and end apart: 17, of which 6 were waited for; matrix products, arithmetic and copies ran while one was open for 0% of the time, Pallas kernels for 3%

profile of v7, /device:TPU:1, one launch (start us, length us, event | category | flops | bytes accessed | tf_op | source)
XLA Modules:
  0.0 172.7 jit_solution(6772996133637497295)
XLA Ops:
  0.6 6.0 %shard_map.30 = bf16[32768,128]{1,0:T(8,128)(2,1)S(1)} custom-call(bf16[1,4194304]{1,0:T(2,128)(2,1)} %x_ref.1), custom_call_target="tpu_custom_call" | custom-call | bytes 25165824 | tf_op jit(solution)/shard_map/pallas_call | solution.py:44
  6.6 105.0 %all_to_all.10.x_ref = bf16[32,1024,128]{2,1,0:T(8,128)(2,1)S(1)} all-to-all(bf16[32,1024,128]{2,1,0:T(8,128)(2,1)S(1)} %bitcast.4), channel_id=1, replica_groups=mesh['rep'=32,'shard'=4] {'rep'}, dimensions={0} | all-to-all | bytes 16777216 | tf_op jit(solution)/shard_map/all_to_all | solution.py:294
  111.6 3.9 %shard_map.31 = f32[4,128]{1,0:T(4,128)S(1)} custom-call(bf16[32,1024,128]{2,1,0:T(8,128)(2,1)S(1)} %all_to_all.10.x_ref), custom_call_target="tpu_custom_call" | custom-call | tf_op jit(solution)/shard_map/pallas_call | solution.py:122
  115.6 17.0 %all_to_all.11.d_ref = f32[128,4,128]{2,1,0:T(4,128)S(1)} all-to-all(f32[128,4,128]{2,1,0:T(4,128)S(1)} %broadcast_in_dim.2), channel_id=1, replica_groups=mesh['rep'=32,'shard'=4] {'rep','shard'}, dimensions={0} | all-to-all | bytes 524288 | tf_op jit(solution)/shard_map/all_to_all | solution.py:297
  132.6 2.6 %shard_map.32 = (bf16[1024,128]{1,0:T(8,128)(2,1)S(1)}, f32[1,128]{1,0:T(1,128)S(1)}) custom-call(f32[128,4,128]{2,1,0:T(4,128)S(1)} %all_to_all.11.d_ref, bf16[32,1024,128]{2,1,0:T(8,128)(2,1)S(1)} %all_to_all.10.x_ref), custom_call_target="tpu_custom_call" | custom-call | tf_op jit(solution)/shard_map/pallas_call | solution.py:192
  135.2 0.1 collective-permute-start
  135.2 2.7 %collective-permute-start.4 = (bf16[1024,128]{1,0:T(8,128)(2,1)S(1)}, bf16[1024,128]{1,0:T(8,128)(2,1)S(1)}, u32[]{:S(2)}, u32[]{:S(2)}) collective-permute-start(bf16[1024,128]{1,0:T(8,128)(2,1)S(1)} %get-tuple-element.8), channel_id=1, source_target_pairs={{0,96},{4,28},{8,104},{12,4},{16,112},{20,12},{24,120},{28,20},{32... | collective-permute-start | bytes 786440 | tf_op jit(solution)/shard_map/ppermute | solution.py:213
  137.9 0.0 collective-permute-start.5
  137.9 4.0 %collective-permute-done = bf16[1024,128]{1,0:T(8,128)(2,1)S(1)} collective-permute-done((bf16[1024,128]{1,0:T(8,128)(2,1)S(1)}, bf16[1024,128]{1,0:T(8,128)(2,1)S(1)}, u32[]{:S(2)}, u32[]{:S(2)}) %collective-permute-start) | collective-permute-done | bytes 262176 | tf_op jit(solution)/shard_map/ppermute | solution.py:213
  142.0 1.2 collective-permute-start.8
  143.2 0.8 collective-permute-done.4
  144.1 0.9 collective-permute-done.5
  145.0 0.1 collective-permute-start.6
  145.1 2.6 %collective-permute-start.1 = (bf16[2048,128]{1,0:T(8,128)(2,1)S(1)}, bf16[2048,128]{1,0:T(8,128)(2,1)S(1)}, u32[]{:S(2)}, u32[]{:S(2)}) collective-permute-start(bf16[2048,128]{1,0:T(8,128)(2,1)S(1)} %constant_dynamic-update-slice_fusion.refs_0_), channel_id=1, source_target_pairs={{0,24},{4,100},{8,0},{12,108},{16,8},{20,116},{24,16},{28,124},{32... | collective-permute-start | bytes 1572872 | tf_op jit(solution)/shard_map/ppermute | solution.py:213
  147.7 2.2 %collective-permute-start.9 = (bf16[2048,128]{1,0:T(8,128)(2,1)S(1)}, bf16[2048,128]{1,0:T(8,128)(2,1)S(1)}, u32[]{:S(2)}, u32[]{:S(2)}) collective-permute-start(bf16[2048,128]{1,0:T(8,128)(2,1)S(1)} %constant_dynamic-update-slice_fusion.2.refs_1_), channel_id=1, source_target_pairs={{0,4},{4,0},{8,12},{12,8},{16,20},{20,16},{24,28},{28,24},{32,36},... | collective-permute-start | bytes 1572872 | tf_op jit(solution)/shard_map/ppermute | solution.py:217
  149.9 2.3 %collective-permute-start.7 = (bf16[2048,128]{1,0:T(8,128)(2,1)S(1)}, bf16[2048,128]{1,0:T(8,128)(2,1)S(1)}, u32[]{:S(2)}, u32[]{:S(2)}) collective-permute-start(bf16[2048,128]{1,0:T(8,128)(2,1)S(1)} %constant_dynamic-update-slice_fusion.2.refs_1_), channel_id=1, source_target_pairs={{0,24},{4,100},{8,0},{12,108},{16,8},{20,116},{24,16},{28,124},{32... | collective-permute-start | bytes 1572872 | tf_op jit(solution)/shard_map/ppermute | solution.py:213
  152.2 0.0 collective-permute-done.8.refs_2_
  152.2 2.3 %collective-permute-done.6.refs_2_ = bf16[2048,128]{1,0:T(8,128)(2,1)S(1)} collective-permute-done((bf16[2048,128]{1,0:T(8,128)(2,1)S(1)}, bf16[2048,128]{1,0:T(8,128)(2,1)S(1)}, u32[]{:S(2)}, u32[]{:S(2)}) %collective-permute-start.6) | collective-permute-done | bytes 524320 | tf_op jit(solution)/shard_map/ppermute | solution.py:213
  154.6 0.5 slice_bitcast_fusion
  155.1 2.7 %collective-permute-start.2 = (bf16[2048,128]{1,0:T(8,128)(2,1)S(1)}, bf16[2048,128]{1,0:T(8,128)(2,1)S(1)}, u32[]{:S(2)}, u32[]{:S(2)}) collective-permute-start(bf16[2048,128]{1,0:T(8,128)(2,1)S(1)} %collective-permute-done.1.refs_1_), channel_id=1, source_target_pairs={{0,24},{4,100},{8,0},{12,108},{16,8},{20,116},{24,16},{28,124},{32... | collective-permute-start | bytes 1572872 | tf_op jit(solution)/shard_map/ppermute | solution.py:213
  157.8 1.4 shard_map.33.refs_4_
  159.1 3.2 %collective-permute-start.15 = (bf16[2048,128]{1,0:T(8,128)(2,1)S(1)}, bf16[2048,128]{1,0:T(8,128)(2,1)S(1)}, u32[]{:S(2)}, u32[]{:S(2)}) collective-permute-start(bf16[2048,128]{1,0:T(8,128)(2,1)S(1)} %collective-permute-done.6.refs_2_), channel_id=1, source_target_pairs={{0,4},{4,0},{8,12},{12,8},{16,20},{20,16},{24,28},{28,24},{32,36},... | collective-permute-start | bytes 1572872 | tf_op jit(solution)/shard_map/ppermute | solution.py:217
  162.3 0.1 collective-permute-start.16
  162.4 0.4 collective-permute-start.14
  162.8 1.4 shard_map.34.refs_6_
  164.2 3.2 %collective-permute-done.11.refs_5_ = bf16[2048,128]{1,0:T(8,128)(2,1)S(1)} collective-permute-done((bf16[2048,128]{1,0:T(8,128)(2,1)S(1)}, bf16[2048,128]{1,0:T(8,128)(2,1)S(1)}, u32[]{:S(2)}, u32[]{:S(2)}) %collective-permute-start.11) | collective-permute-done | bytes 524320 | tf_op jit(solution)/shard_map/ppermute | solution.py:213
  167.4 1.0 collective-permute-start.13
  168.3 0.0 collective-permute-start.12
  168.4 0.5 collective-permute-start.10
  168.9 1.0 collective-permute-done.13.refs_0_
  169.9 1.8 %shard_map.35.refs_2_ = bf16[32768,128]{1,0:T(8,128)(2,1)} custom-call(bf16[2048,128]{1,0:T(8,128)(2,1)S(1)} %collective-permute-done.13.refs_0_, bf16[2048,128]{1,0:T(8,128)(2,1)S(1)} %collective-permute-done.14.refs_1_, bf16[2048,128]{1,0:T(8,128)(2,1)S(1)} %collective-permute-done.15.refs_2_, ...), custom_call_target="tpu_custom_call", output_to_operand_aliasing={{}: (6, {})} | custom-call | bytes 3145728 | tf_op jit(solution)/shard_map/pallas_call | solution.py:242
  171.7 1.0 shard_map.36
  (17 shorter events, 0.2 us)
Async XLA Ops:
  135.2 6.8 %collective-permute-start = (bf16[1024,128]{1,0:T(8,128)(2,1)S(1)}, bf16[1024,128]{1,0:T(8,128)(2,1)S(1)}, u32[]{:S(2)}, u32[]{:S(2)}) collective-permute-start(bf16[1024,128]{1,0:T(8,128)(2,1)S(1)} %get-tuple-element.8), channel_id=1, source_target_pairs={{0,32},{4,12},{8,40},{12,20},{16,48},{20,28},{24,56},{28,4},{32,64... | collective-permute-start | bytes 786440 | tf_op jit(solution)/shard_map/ppermute | solution.py:213
  135.2 8.8 %collective-permute-start.4 = (bf16[1024,128]{1,0:T(8,128)(2,1)S(1)}, bf16[1024,128]{1,0:T(8,128)(2,1)S(1)}, u32[]{:S(2)}, u32[]{:S(2)}) collective-permute-start(bf16[1024,128]{1,0:T(8,128)(2,1)S(1)} %get-tuple-element.8), channel_id=1, source_target_pairs={{0,96},{4,28},{8,104},{12,4},{16,112},{20,12},{24,120},{28,20},{32... | collective-permute-start | bytes 786440 | tf_op jit(solution)/shard_map/ppermute | solution.py:213
  137.9 7.0 %collective-permute-start.5 = (bf16[1024,128]{1,0:T(8,128)(2,1)S(1)}, bf16[1024,128]{1,0:T(8,128)(2,1)S(1)}, u32[]{:S(2)}, u32[]{:S(2)}) collective-permute-start(bf16[1024,128]{1,0:T(8,128)(2,1)S(1)} %get-tuple-element.8), channel_id=1, source_target_pairs={{0,64},{4,20},{8,72},{12,28},{16,80},{20,4},{24,88},{28,12},{32,96... | collective-permute-start | bytes 786440 | tf_op jit(solution)/shard_map/ppermute | solution.py:213
  142.0 10.2 %collective-permute-start.8 = (bf16[2048,128]{1,0:T(8,128)(2,1)S(1)}, bf16[2048,128]{1,0:T(8,128)(2,1)S(1)}, u32[]{:S(2)}, u32[]{:S(2)}) collective-permute-start(bf16[2048,128]{1,0:T(8,128)(2,1)S(1)} %constant_dynamic-update-slice_fusion.refs_0_), channel_id=1, source_target_pairs={{0,4},{4,0},{8,12},{12,8},{16,20},{20,16},{24,28},{28,24},{32,36},... | collective-permute-start | bytes 1572872 | tf_op jit(solution)/shard_map/ppermute | solution.py:217
  145.0 9.6 %collective-permute-start.6 = (bf16[2048,128]{1,0:T(8,128)(2,1)S(1)}, bf16[2048,128]{1,0:T(8,128)(2,1)S(1)}, u32[]{:S(2)}, u32[]{:S(2)}) collective-permute-start(bf16[2048,128]{1,0:T(8,128)(2,1)S(1)} %constant_dynamic-update-slice_fusion.2.refs_1_), channel_id=1, source_target_pairs={{0,8},{4,36},{8,16},{12,44},{16,24},{20,52},{24,0},{28,60},{32,40}... | collective-permute-start | bytes 1572872 | tf_op jit(solution)/shard_map/ppermute | solution.py:213
  145.1 10.0 %collective-permute-start.1 = (bf16[2048,128]{1,0:T(8,128)(2,1)S(1)}, bf16[2048,128]{1,0:T(8,128)(2,1)S(1)}, u32[]{:S(2)}, u32[]{:S(2)}) collective-permute-start(bf16[2048,128]{1,0:T(8,128)(2,1)S(1)} %constant_dynamic-update-slice_fusion.refs_0_), channel_id=1, source_target_pairs={{0,24},{4,100},{8,0},{12,108},{16,8},{20,116},{24,16},{28,124},{32... | collective-permute-start | bytes 1572872 | tf_op jit(solution)/shard_map/ppermute | solution.py:213
  147.7 10.1 %collective-permute-start.9 = (bf16[2048,128]{1,0:T(8,128)(2,1)S(1)}, bf16[2048,128]{1,0:T(8,128)(2,1)S(1)}, u32[]{:S(2)}, u32[]{:S(2)}) collective-permute-start(bf16[2048,128]{1,0:T(8,128)(2,1)S(1)} %constant_dynamic-update-slice_fusion.2.refs_1_), channel_id=1, source_target_pairs={{0,4},{4,0},{8,12},{12,8},{16,20},{20,16},{24,28},{28,24},{32,36},... | collective-permute-start | bytes 1572872 | tf_op jit(solution)/shard_map/ppermute | solution.py:217
  149.9 12.4 %collective-permute-start.7 = (bf16[2048,128]{1,0:T(8,128)(2,1)S(1)}, bf16[2048,128]{1,0:T(8,128)(2,1)S(1)}, u32[]{:S(2)}, u32[]{:S(2)}) collective-permute-start(bf16[2048,128]{1,0:T(8,128)(2,1)S(1)} %constant_dynamic-update-slice_fusion.2.refs_1_), channel_id=1, source_target_pairs={{0,24},{4,100},{8,0},{12,108},{16,8},{20,116},{24,16},{28,124},{32... | collective-permute-start | bytes 1572872 | tf_op jit(solution)/shard_map/ppermute | solution.py:213
  152.2 10.2 %collective-permute-start.3 = (bf16[2048,128]{1,0:T(8,128)(2,1)S(1)}, bf16[2048,128]{1,0:T(8,128)(2,1)S(1)}, u32[]{:S(2)}, u32[]{:S(2)}) collective-permute-start(bf16[2048,128]{1,0:T(8,128)(2,1)S(1)} %constant_dynamic-update-slice_fusion.refs_0_), channel_id=1, source_target_pairs={{0,8},{4,36},{8,16},{12,44},{16,24},{20,52},{24,0},{28,60},{32,40}... | collective-permute-start | bytes 1572872 | tf_op jit(solution)/shard_map/ppermute | solution.py:213
  154.6 12.8 %collective-permute-start.11 = (bf16[2048,128]{1,0:T(8,128)(2,1)S(1)}, bf16[2048,128]{1,0:T(8,128)(2,1)S(1)}, u32[]{:S(2)}, u32[]{:S(2)}) collective-permute-start(bf16[2048,128]{1,0:T(8,128)(2,1)S(1)} %collective-permute-done.6.refs_2_), channel_id=1, source_target_pairs={{0,8},{4,36},{8,16},{12,44},{16,24},{20,52},{24,0},{28,60},{32,40}... | collective-permute-start | bytes 1572872 | tf_op jit(solution)/shard_map/ppermute | solution.py:213
  155.1 13.3 %collective-permute-start.2 = (bf16[2048,128]{1,0:T(8,128)(2,1)S(1)}, bf16[2048,128]{1,0:T(8,128)(2,1)S(1)}, u32[]{:S(2)}, u32[]{:S(2)}) collective-permute-start(bf16[2048,128]{1,0:T(8,128)(2,1)S(1)} %collective-permute-done.1.refs_1_), channel_id=1, source_target_pairs={{0,24},{4,100},{8,0},{12,108},{16,8},{20,116},{24,16},{28,124},{32... | collective-permute-start | bytes 1572872 | tf_op jit(solution)/shard_map/ppermute | solution.py:213
  159.1 9.2 %collective-permute-start.15 = (bf16[2048,128]{1,0:T(8,128)(2,1)S(1)}, bf16[2048,128]{1,0:T(8,128)(2,1)S(1)}, u32[]{:S(2)}, u32[]{:S(2)}) collective-permute-start(bf16[2048,128]{1,0:T(8,128)(2,1)S(1)} %collective-permute-done.6.refs_2_), channel_id=1, source_target_pairs={{0,4},{4,0},{8,12},{12,8},{16,20},{20,16},{24,28},{28,24},{32,36},... | collective-permute-start | bytes 1572872 | tf_op jit(solution)/shard_map/ppermute | solution.py:217
  162.3 6.5 %collective-permute-start.16 = (bf16[2048,128]{1,0:T(8,128)(2,1)S(1)}, bf16[2048,128]{1,0:T(8,128)(2,1)S(1)}, u32[]{:S(2)}, u32[]{:S(2)}) collective-permute-start(bf16[2048,128]{1,0:T(8,128)(2,1)S(1)} %collective-permute-done.7.refs_3_), channel_id=1, source_target_pairs={{0,4},{4,0},{8,12},{12,8},{16,20},{20,16},{24,28},{28,24},{32,36},... | collective-permute-start | bytes 1572872 | tf_op jit(solution)/shard_map/ppermute | solution.py:217
  162.4 6.4 %collective-permute-start.14 = (bf16[2048,128]{1,0:T(8,128)(2,1)S(1)}, bf16[2048,128]{1,0:T(8,128)(2,1)S(1)}, u32[]{:S(2)}, u32[]{:S(2)}) collective-permute-start(bf16[2048,128]{1,0:T(8,128)(2,1)S(1)} %collective-permute-done.1.refs_1_), channel_id=1, source_target_pairs={{0,4},{4,0},{8,12},{12,8},{16,20},{20,16},{24,28},{28,24},{32,36},... | collective-permute-start | bytes 1572872 | tf_op jit(solution)/shard_map/ppermute | solution.py:217
  167.4 2.5 %collective-permute-start.13 = (bf16[2048,128]{1,0:T(8,128)(2,1)S(1)}, bf16[2048,128]{1,0:T(8,128)(2,1)S(1)}, u32[]{:S(2)}, u32[]{:S(2)}) collective-permute-start(bf16[2048,128]{1,0:T(8,128)(2,1)S(1)} %collective-permute-done.3.refs_0_), channel_id=1, source_target_pairs={{0,4},{4,0},{8,12},{12,8},{16,20},{20,16},{24,28},{28,24},{32,36},... | collective-permute-start | bytes 1572872 | tf_op jit(solution)/shard_map/ppermute | solution.py:217
  168.3 3.3 %collective-permute-start.12 = (bf16[2048,128]{1,0:T(8,128)(2,1)S(1)}, bf16[2048,128]{1,0:T(8,128)(2,1)S(1)}, u32[]{:S(2)}, u32[]{:S(2)}) collective-permute-start(bf16[2048,128]{1,0:T(8,128)(2,1)S(1)} %collective-permute-done.11.refs_5_), channel_id=1, source_target_pairs={{0,4},{4,0},{8,12},{12,8},{16,20},{20,16},{24,28},{28,24},{32,36},... | collective-permute-start | bytes 1572872 | tf_op jit(solution)/shard_map/ppermute | solution.py:217
  168.4 3.3 %collective-permute-start.10 = (bf16[2048,128]{1,0:T(8,128)(2,1)S(1)}, bf16[2048,128]{1,0:T(8,128)(2,1)S(1)}, u32[]{:S(2)}, u32[]{:S(2)}) collective-permute-start(bf16[2048,128]{1,0:T(8,128)(2,1)S(1)} %collective-permute-done.2.refs_4_), channel_id=1, source_target_pairs={{0,4},{4,0},{8,12},{12,8},{16,20},{20,16},{24,28},{28,24},{32,36},... | collective-permute-start | bytes 1572872 | tf_op jit(solution)/shard_map/ppermute | solution.py:217
